TPU v7x, 32 devices: a whole 2x2x4 slice. The times are simulated.
32 devices in a mesh: seq: 8 (over y, x, core), head: 4 (over z).
Axes of the slice: x: 2, y: 2, z: 4, core: 2. Of those that a mesh axis runs over, the one named last changes fastest.
Arguments:
- inputs_x: bfloat16 [2048, 8192], P('seq', 'head'), may hold values from -6 to 6
- inputs_b: bfloat16 [2048, 1024], P('seq', 'head'), may hold values from -0.59765625 to 0.59765625
- inputs_c: bfloat16 [2048, 1024], P('seq', 'head'), may hold values from -6 to 6
- gate_z: bfloat16 [2048, 8192], P('seq', 'head'), may hold values from -6 to 6
- log_decay: float32 [128, 2048], P('head', 'seq'), may hold values from -1 to 0, as said below
- resets: int32 [2048], P('seq'), may hold values from 0 to 1, as said below
- norm_gain: float32 [8192], P('head'), may hold values from 0.1 to 1.9
- out_weight: bfloat16 [4096, 8192], P('seq', 'head'), may hold values from -0.09375 to 0.09375
- out_grad: bfloat16 [2048, 4096], P('seq', 'head'), may hold values from -6 to 6
Outputs:
- layer_out: bfloat16 [2048, 4096], P('seq', 'head')
- grad_x: float32 [2048, 8192], P('seq', 'head')
- grad_b: float32 [2048, 1024], P('seq', 'head')
- grad_c: float32 [2048, 1024], P('seq', 'head')
- grad_z: float32 [2048, 8192], P('seq', 'head')
- grad_decay: float32 [128, 2048], P('head', 'seq')
- grad_weight: float32 [4096, 8192], P('seq', 'head')
Inputs may be any that keep to these rules, and one draw needn't show every extreme that they name: `log_decay`: the decay factor of a token is exp of its entry. `resets`: exactly one entry is 1, the first token of the second rollout, at a position from 256 to 1791.
All inputs are finite; a program needn't handle non-finite values.
Results may differ from a plain program's by a relative error of at most 0.023.
Values may be sent and summed in bfloat16 or wider, within the bound.
A program may use at most 128 MiB of HBM per device.

v0:
```python
import jax
import jax.numpy as jnp
from jax import lax
from jax.sharding import PartitionSpec as P

P_SIZE = 64
N = 128
G = 8
SPAN = 256
HP = 8192


def from_behind(value, axis, steps):
    count = lax.axis_size(axis)
    leading, last = (max(0, -steps), min(count, count - steps))
    return lax.ppermute(value, axis, [(source, source + steps) for source in range(leading, last)])


def span_scan(inputs_x, inputs_b, inputs_c, log_decay, resets, start_state):
    tokens_here = inputs_x.shape[0]
    heads_here = log_decay.shape[0]
    groups_here = inputs_b.shape[1] // N
    repeat_count = heads_here // groups_here
    blocks = tokens_here // SPAN
    x_blocks = inputs_x.reshape(blocks, SPAN, heads_here, P_SIZE)
    b_blocks = inputs_b.reshape(blocks, SPAN, groups_here, N)
    c_blocks = inputs_c.reshape(blocks, SPAN, groups_here, N)
    d_blocks = log_decay.reshape(heads_here, blocks, SPAN).transpose(1, 0, 2)
    r_blocks = resets.reshape(blocks, SPAN)
    order = jnp.arange(SPAN, dtype=jnp.int32)
    lower = order[None, :] <= order[:, None]

    def advance(state, pieces):
        x_here, b_here, c_here, d_here, r_here = pieces
        cumul = jnp.cumsum(d_here, axis=1)
        counts = jnp.cumsum(r_here)
        same = lower & (counts[:, None] == counts[None, :])
        spread = cumul[:, :, None] - cumul[:, None, :]
        weights = jnp.where(same[None], jnp.exp(jnp.minimum(spread, 0.0)), 0.0)
        scores = jnp.einsum("tgn,sgn->gts", c_here, b_here, precision=lax.Precision.HIGHEST)
        scores = jnp.repeat(scores, repeat_count, axis=0) * weights
        inner = jnp.einsum("hts,shp->thp", scores, x_here, precision=lax.Precision.HIGHEST)
        c_heads = jnp.repeat(c_here, repeat_count, axis=1)
        b_heads = jnp.repeat(b_here, repeat_count, axis=1)
        entry = jnp.exp(cumul) * (counts == 0).astype(jnp.float32)[None, :]
        carried = (
            jnp.einsum("thn,hpn->thp", c_heads, state, precision=lax.Precision.HIGHEST)
            * entry.T[:, :, None]
        )
        tail = jnp.exp(cumul[:, -1:] - cumul) * (counts == counts[-1]).astype(jnp.float32)[None, :]
        fresh = jnp.einsum(
            "shp,shn->hpn", x_here * tail.T[:, :, None], b_heads, precision=lax.Precision.HIGHEST
        )
        passing = entry[:, -1]
        return (fresh + passing[:, None, None] * state, inner + carried)

    final, outputs = lax.scan(
        jax.checkpoint(advance), start_state, (x_blocks, b_blocks, c_blocks, d_blocks, r_blocks)
    )
    return (outputs.reshape(tokens_here, heads_here * P_SIZE), final)


def gated_norm(values, gate, gain):
    gated = values * jax.nn.silu(gate)
    rows_here, width = gated.shape
    group_width = HP // G
    grouped = gated.reshape(rows_here, width // group_width, group_width)
    scale = lax.rsqrt(jnp.mean(grouped * grouped, axis=2, keepdims=True) + 1e-05)
    return (grouped * scale).reshape(rows_here, width) * gain[None, :]


def carried_term(inputs_c, log_decay, resets, state):
    heads_here = log_decay.shape[0]
    tokens_here = inputs_c.shape[0]
    groups_here = inputs_c.shape[1] // N
    cumul = jnp.cumsum(log_decay, axis=1)
    counts = jnp.cumsum(resets)
    entry = jnp.exp(cumul) * (counts == 0).astype(jnp.float32)[None, :]
    c_heads = jnp.repeat(
        inputs_c.reshape(tokens_here, groups_here, N), heads_here // groups_here, axis=1
    )
    result = (
        jnp.einsum("thn,hpn->thp", c_heads, state, precision=lax.Precision.HIGHEST)
        * entry.T[:, :, None]
    )
    return result.reshape(tokens_here, heads_here * P_SIZE)


def device_decay(log_decay, resets):
    return jnp.exp(jnp.sum(log_decay, axis=1)) * (jnp.sum(resets) == 0).astype(jnp.float32)


def per_device(
    inputs_x, inputs_b, inputs_c, gate_z, log_decay, resets, norm_gain, out_weight, out_grad
):
    x_float = inputs_x.astype(jnp.float32)
    b_float = inputs_b.astype(jnp.float32)
    c_float = inputs_c.astype(jnp.float32)
    z_float = gate_z.astype(jnp.float32)
    heads_here = log_decay.shape[0]
    zero_state = jnp.zeros((heads_here, P_SIZE, N), jnp.float32)

    def local_scan(x_arg, b_arg, c_arg, decay_arg):
        return span_scan(x_arg, b_arg, c_arg, decay_arg, resets, zero_state)

    (y_zero, s_local), pull_scan = jax.vjp(local_scan, x_float, b_float, c_float, log_decay)

    def whole_decay(decay_arg):
        return device_decay(decay_arg, resets)

    g_local, pull_decay = jax.vjp(whole_decay, log_decay)

    def forward_step(turn, carried):
        return from_behind(
            (g_local[:, None, None] * carried + s_local).astype(jnp.bfloat16), "seq", 1
        ).astype(jnp.float32)

    state_in = lax.fori_loop(0, lax.axis_size("seq") - 1, forward_step, zero_state)

    def finish(y_arg, c_arg, decay_arg, z_arg, state_arg):
        return gated_norm(
            y_arg + carried_term(c_arg, decay_arg, resets, state_arg), z_arg, norm_gain
        )

    normed, pull_finish = jax.vjp(finish, y_zero, c_float, log_decay, z_float, state_in)
    normed_bf = normed.astype(jnp.bfloat16)
    full_weight = lax.all_gather(out_weight, "seq", axis=0, tiled=True)
    partial_value = lax.dot_general(
        normed_bf, full_weight, (((1,), (1,)), ((), ())), preferred_element_type=jnp.float32
    )
    layer_out = lax.psum_scatter(
        partial_value.astype(jnp.bfloat16), "head", scatter_dimension=1, tiled=True
    )
    grad_full = lax.all_gather(out_grad, "head", axis=1, tiled=True)
    grad_y = jnp.dot(grad_full, full_weight, preferred_element_type=jnp.float32)
    grad_weight = lax.psum_scatter(
        lax.dot_general(
            grad_full, normed_bf, (((0,), (0,)), ((), ())), preferred_element_type=jnp.float32
        ).astype(jnp.bfloat16),
        "seq",
        scatter_dimension=0,
        tiled=True,
    ).astype(jnp.float32)
    d_zero, d_c_two, d_decay_two, grad_z, adjoint_in = pull_finish(grad_y)

    def backward_step(turn, carried):
        return from_behind(
            (g_local[:, None, None] * carried + adjoint_in).astype(jnp.bfloat16), "seq", -1
        ).astype(jnp.float32)

    adjoint_out = lax.fori_loop(0, lax.axis_size("seq") - 1, backward_step, zero_state)
    grad_x, grad_b, d_c_one, d_decay_one = pull_scan((d_zero, adjoint_out))
    (d_decay_three,) = pull_decay(jnp.sum(adjoint_out * state_in, axis=(1, 2)))
    return (
        layer_out,
        grad_x,
        grad_b,
        d_c_one + d_c_two,
        grad_z,
        d_decay_one + d_decay_two + d_decay_three,
        grad_weight,
    )


def solution(mesh):
    return jax.shard_map(
        per_device,
        mesh=mesh,
        in_specs=(
            P("seq", "head"),
            P("seq", "head"),
            P("seq", "head"),
            P("seq", "head"),
            P("head", "seq"),
            P("seq"),
            P("head"),
            P("seq", "head"),
            P("seq", "head"),
        ),
        out_specs=(
            P("seq", "head"),
            P("seq", "head"),
            P("seq", "head"),
            P("seq", "head"),
            P("seq", "head"),
            P("head", "seq"),
            P("seq", "head"),
        ),
        check_vma=False,
    )
```

profile of v0, /device:TPU:11, one launch (start us, length us, event | category | flops | bytes accessed | tf_op | source)
XLA Modules:
  0.0 508.0 jit_solution(9916616868889643203)
XLA Ops:
  24.4 129.5 %while.6 = (s32[]{:T(128)}, f32[32,64,128]{2,1,0:T(8,128)S(1)}, f32[32]{0:T(128)S(1)}, f32[32,64,128]{2,1,0:T(8,128)S(1)}, s32[]{:T(128)}, /*index=5*/s32[]{:T(128)}) while((s32[]{:T(128)}, f32[32,64,128]{2,1,0:T(8,128)S(1)}, f32[32]{0:T(128)S(1)}, f32[32,64,128]{2,1,0:T(8,128)S(1)}, s32[]{:T(128)}, /*index=5*/s32[]{:T(128)}) %tuple.73), condition=%wide.region_7.8_spmd.clone, body=%wide.region_6.7_spmd.clone.sunk | while | flops 1310723 | bytes 6291703 | solution.py:118
  29.1 6.4 %collective-permute-done = bf16[32,64,128]{2,1,0:T(8,128)(2,1)} collective-permute-done((bf16[32,64,128]{2,1,0:T(8,128)(2,1)}, bf16[32,64,128]{2,1,0:T(8,128)(2,1)}, u32[]{:S(2)}, u32[]{:S(2)}) %collective-permute-start) | collective-permute-done | bytes 524320 | tf_op jit(solution)/shard_map/while/body/eval_jaxpr/ppermute | solution.py:16
  43.0 6.4 %collective-permute-done = bf16[32,64,128]{2,1,0:T(8,128)(2,1)} collective-permute-done((bf16[32,64,128]{2,1,0:T(8,128)(2,1)}, bf16[32,64,128]{2,1,0:T(8,128)(2,1)}, u32[]{:S(2)}, u32[]{:S(2)}) %collective-permute-start) | collective-permute-done | bytes 524320 | tf_op jit(solution)/shard_map/while/body/eval_jaxpr/ppermute | solution.py:16
  51.5 5.3 %collective-permute-start = (bf16[32,64,128]{2,1,0:T(8,128)(2,1)}, bf16[32,64,128]{2,1,0:T(8,128)(2,1)}, u32[]{:S(2)}, u32[]{:S(2)}) collective-permute-start(bf16[32,64,128]{2,1,0:T(8,128)(2,1)} %fusion.114), channel_id=1, source_target_pairs={{0,4},{4,8},{8,12},{12,16},{16,20},{20,24},{24,28},{1,5},{5,9},{9,... | collective-permute-start | bytes 1572872 | tf_op jit(solution)/shard_map/while/body/eval_jaxpr/ppermute | solution.py:16
  56.8 6.4 %collective-permute-done = bf16[32,64,128]{2,1,0:T(8,128)(2,1)} collective-permute-done((bf16[32,64,128]{2,1,0:T(8,128)(2,1)}, bf16[32,64,128]{2,1,0:T(8,128)(2,1)}, u32[]{:S(2)}, u32[]{:S(2)}) %collective-permute-start) | collective-permute-done | bytes 524320 | tf_op jit(solution)/shard_map/while/body/eval_jaxpr/ppermute | solution.py:16
  65.4 5.4 %collective-permute-start = (bf16[32,64,128]{2,1,0:T(8,128)(2,1)}, bf16[32,64,128]{2,1,0:T(8,128)(2,1)}, u32[]{:S(2)}, u32[]{:S(2)}) collective-permute-start(bf16[32,64,128]{2,1,0:T(8,128)(2,1)} %fusion.114), channel_id=1, source_target_pairs={{0,4},{4,8},{8,12},{12,16},{16,20},{20,24},{24,28},{1,5},{5,9},{9,... | collective-permute-start | bytes 1572872 | tf_op jit(solution)/shard_map/while/body/eval_jaxpr/ppermute | solution.py:16
  70.8 17.6 %collective-permute-done = bf16[32,64,128]{2,1,0:T(8,128)(2,1)} collective-permute-done((bf16[32,64,128]{2,1,0:T(8,128)(2,1)}, bf16[32,64,128]{2,1,0:T(8,128)(2,1)}, u32[]{:S(2)}, u32[]{:S(2)}) %collective-permute-start) | collective-permute-done | bytes 524320 | tf_op jit(solution)/shard_map/while/body/eval_jaxpr/ppermute | solution.py:16
  90.6 5.3 %collective-permute-start = (bf16[32,64,128]{2,1,0:T(8,128)(2,1)}, bf16[32,64,128]{2,1,0:T(8,128)(2,1)}, u32[]{:S(2)}, u32[]{:S(2)}) collective-permute-start(bf16[32,64,128]{2,1,0:T(8,128)(2,1)} %fusion.114), channel_id=1, source_target_pairs={{0,4},{4,8},{8,12},{12,16},{16,20},{20,24},{24,28},{1,5},{5,9},{9,... | collective-permute-start | bytes 1572872 | tf_op jit(solution)/shard_map/while/body/eval_jaxpr/ppermute | solution.py:16
  95.9 6.4 %collective-permute-done = bf16[32,64,128]{2,1,0:T(8,128)(2,1)} collective-permute-done((bf16[32,64,128]{2,1,0:T(8,128)(2,1)}, bf16[32,64,128]{2,1,0:T(8,128)(2,1)}, u32[]{:S(2)}, u32[]{:S(2)}) %collective-permute-start) | collective-permute-done | bytes 524320 | tf_op jit(solution)/shard_map/while/body/eval_jaxpr/ppermute | solution.py:16
  104.5 5.4 %collective-permute-start = (bf16[32,64,128]{2,1,0:T(8,128)(2,1)}, bf16[32,64,128]{2,1,0:T(8,128)(2,1)}, u32[]{:S(2)}, u32[]{:S(2)}) collective-permute-start(bf16[32,64,128]{2,1,0:T(8,128)(2,1)} %fusion.114), channel_id=1, source_target_pairs={{0,4},{4,8},{8,12},{12,16},{16,20},{20,24},{24,28},{1,5},{5,9},{9,... | collective-permute-start | bytes 1572872 | tf_op jit(solution)/shard_map/while/body/eval_jaxpr/ppermute | solution.py:16
  109.9 17.6 %collective-permute-done = bf16[32,64,128]{2,1,0:T(8,128)(2,1)} collective-permute-done((bf16[32,64,128]{2,1,0:T(8,128)(2,1)}, bf16[32,64,128]{2,1,0:T(8,128)(2,1)}, u32[]{:S(2)}, u32[]{:S(2)}) %collective-permute-start) | collective-permute-done | bytes 524320 | tf_op jit(solution)/shard_map/while/body/eval_jaxpr/ppermute | solution.py:16
  129.7 5.3 %collective-permute-start = (bf16[32,64,128]{2,1,0:T(8,128)(2,1)}, bf16[32,64,128]{2,1,0:T(8,128)(2,1)}, u32[]{:S(2)}, u32[]{:S(2)}) collective-permute-start(bf16[32,64,128]{2,1,0:T(8,128)(2,1)} %fusion.114), channel_id=1, source_target_pairs={{0,4},{4,8},{8,12},{12,16},{16,20},{20,24},{24,28},{1,5},{5,9},{9,... | collective-permute-start | bytes 1572872 | tf_op jit(solution)/shard_map/while/body/eval_jaxpr/ppermute | solution.py:16
  135.0 17.6 %collective-permute-done = bf16[32,64,128]{2,1,0:T(8,128)(2,1)} collective-permute-done((bf16[32,64,128]{2,1,0:T(8,128)(2,1)}, bf16[32,64,128]{2,1,0:T(8,128)(2,1)}, u32[]{:S(2)}, u32[]{:S(2)}) %collective-permute-start) | collective-permute-done | bytes 524320 | tf_op jit(solution)/shard_map/while/body/eval_jaxpr/ppermute | solution.py:16
  160.2 8.6 %fusion.76 = f32[32,256,64]{1,2,0:T(8,128)S(1)} fusion(f32[32,256,256]{2,1,0:T(8,128)} %bitcast_multiply_fusion.2, bf16[256,32,64]{0,2,1:T(8,128)(2,1)S(1)} %bitcast.249), kind=kOutput, calls=%fused_computation.138 | convolution fusion | flops 1610612736 | bytes 11534336 | tf_op jit(solution)/shard_map/jvp()/while/body/eval_jaxpr/hts,shp->thp/dot_general | solution.py:42
  168.9 6.0 %fusion.27 = f32[256,32,64]{0,2,1:T(8,128)} fusion(f32[32,64,256]{2,1,0:T(8,128)S(1)} %fusion.77, f32[32,256,64]{1,2,0:T(8,128)S(1)} %fusion.76, f32[256,32,128]{2,0,1:T(8,128)S(1)} %bitcast.243, f32[256,32]{0,1:T(8,128)S(1)} %bitcast.265), kind=kOutput, calls=%fused_computation.53 | convolution fusion | flops 807403520 | bytes 10518528 | tf_op jit(solution)/shard_map/jvp()/while/body/eval_jaxpr/thn,hpn->thp/dot_general | solution.py:47
  177.0 14.1 %fusion.73 = (f32[256,2048]{1,0:T(8,128)}, f32[256,2048]{1,0:T(8,128)}, f32[256,2048]{1,0:T(8,128)}) fusion(f32[256,2048]{1,0:T(8,128)S(1)} %copy.169, bf16[256,2048]{1,0:T(8,128)(2,1)} %param.16, f32[2048]{0:T(1024)S(1)} %copy-done.37, bf16[256,4096]{1,0:T(8,128)(2,1)} %all-gather.5.cloned.1.call-done, bf16[4096,2048]{1,0:T(8,128)(2,1)} %all-gather.3.cloned.1.call-done), kind=kOutput, calls=%fused_computation.135 | convolution fusion | flops 4299685888 | bytes 28319744 | tf_op jit(solution)/shard_map/dot_general | solution.py:135
  217.5 12.2 %convert_bitcast_fusion = bf16[4096,2048]{0,1:T(8,128)(2,1)} fusion(bf16[256,2048]{1,0:T(8,128)(2,1)} %get-tuple-element.242, bf16[256,4096]{1,0:T(8,128)(2,1)} %all-gather.5.cloned.1.call-done), kind=kOutput, calls=%fused_computation.6 | convolution fusion | flops 4303355904 | bytes 19922944 | tf_op jit(solution)/shard_map/dot_general | solution.py:137
  234.8 6.1 %fusion.25 = f32[32,64,128]{2,1,0:T(8,128)} fusion(f32[256,32,128]{2,0,1:T(8,128)} %bitcast.244, f32[256,32,64]{0,2,1:T(8,128)S(1)} %bitcast.236, f32[256,32]{0,1:T(8,128)S(1)} %bitcast.266), kind=kOutput, calls=%fused_computation.49 | convolution fusion | flops 805830656 | bytes 7372800 | tf_op jit(solution)/shard_map/transpose(jvp(thn,hpn->thp))/dot_general | solution.py:83
  240.9 145.9 %while.7 = (s32[]{:T(128)}, f32[32,64,128]{2,1,0:T(8,128)S(1)}, f32[32]{0:T(128)S(1)}, f32[32,64,128]{2,1,0:T(8,128)}, s32[]{:T(128)}, /*index=5*/s32[]{:T(128)}) while((s32[]{:T(128)}, f32[32,64,128]{2,1,0:T(8,128)S(1)}, f32[32]{0:T(128)S(1)}, f32[32,64,128]{2,1,0:T(8,128)}, s32[]{:T(128)}, /*index=5*/s32[]{:T(128)}) %tuple.87), condition=%wide.region_12.13_spmd.clone, body=%wide.region_11.12_spmd.clone.sunk | while | flops 1310723 | bytes 6291703 | solution.py:151
  245.2 11.1 %collective-permute-done.1 = bf16[32,64,128]{2,1,0:T(8,128)(2,1)} collective-permute-done((bf16[32,64,128]{2,1,0:T(8,128)(2,1)}, bf16[32,64,128]{2,1,0:T(8,128)(2,1)}, u32[]{:S(2)}, u32[]{:S(2)}) %collective-permute-start.1) | collective-permute-done | bytes 524320 | tf_op jit(solution)/shard_map/while/body/eval_jaxpr/ppermute | solution.py:16
  261.9 13.0 %collective-permute-done.1 = bf16[32,64,128]{2,1,0:T(8,128)(2,1)} collective-permute-done((bf16[32,64,128]{2,1,0:T(8,128)(2,1)}, bf16[32,64,128]{2,1,0:T(8,128)(2,1)}, u32[]{:S(2)}, u32[]{:S(2)}) %collective-permute-start.1) | collective-permute-done | bytes 524320 | tf_op jit(solution)/shard_map/while/body/eval_jaxpr/ppermute | solution.py:16
  280.3 21.0 %collective-permute-done.1 = bf16[32,64,128]{2,1,0:T(8,128)(2,1)} collective-permute-done((bf16[32,64,128]{2,1,0:T(8,128)(2,1)}, bf16[32,64,128]{2,1,0:T(8,128)(2,1)}, u32[]{:S(2)}, u32[]{:S(2)}) %collective-permute-start.1) | collective-permute-done | bytes 524320 | tf_op jit(solution)/shard_map/while/body/eval_jaxpr/ppermute | solution.py:16
  306.6 21.0 %collective-permute-done.1 = bf16[32,64,128]{2,1,0:T(8,128)(2,1)} collective-permute-done((bf16[32,64,128]{2,1,0:T(8,128)(2,1)}, bf16[32,64,128]{2,1,0:T(8,128)(2,1)}, u32[]{:S(2)}, u32[]{:S(2)}) %collective-permute-start.1) | collective-permute-done | bytes 524320 | tf_op jit(solution)/shard_map/while/body/eval_jaxpr/ppermute | solution.py:16
  332.9 20.8 %collective-permute-done.1 = bf16[32,64,128]{2,1,0:T(8,128)(2,1)} collective-permute-done((bf16[32,64,128]{2,1,0:T(8,128)(2,1)}, bf16[32,64,128]{2,1,0:T(8,128)(2,1)}, u32[]{:S(2)}, u32[]{:S(2)}) %collective-permute-start.1) | collective-permute-done | bytes 524320 | tf_op jit(solution)/shard_map/while/body/eval_jaxpr/ppermute | solution.py:16
  359.0 11.5 %collective-permute-done.1 = bf16[32,64,128]{2,1,0:T(8,128)(2,1)} collective-permute-done((bf16[32,64,128]{2,1,0:T(8,128)(2,1)}, bf16[32,64,128]{2,1,0:T(8,128)(2,1)}, u32[]{:S(2)}, u32[]{:S(2)}) %collective-permute-start.1) | collective-permute-done | bytes 524320 | tf_op jit(solution)/shard_map/while/body/eval_jaxpr/ppermute | solution.py:16
  375.8 9.8 %collective-permute-done.1 = bf16[32,64,128]{2,1,0:T(8,128)(2,1)} collective-permute-done((bf16[32,64,128]{2,1,0:T(8,128)(2,1)}, bf16[32,64,128]{2,1,0:T(8,128)(2,1)}, u32[]{:S(2)}, u32[]{:S(2)}) %collective-permute-start.1) | collective-permute-done | bytes 524320 | tf_op jit(solution)/shard_map/while/body/eval_jaxpr/ppermute | solution.py:16
  396.1 6.0 %fusion.22 = (f32[256,32]{0,1:T(8,128)S(1)}, f32[32,64,256]{2,1,0:T(8,128)}) fusion(f32[256,32,64]{0,2,1:T(8,128)S(1)} %copy-done.2, f32[32,64,128]{2,1,0:T(8,128)S(1)} %get-tuple-element.137, f32[256,32,128]{2,0,1:T(8,128)S(1)} %bitcast.247), kind=kOutput, calls=%fused_computation.46 | convolution fusion | flops 806346752 | bytes 9469952 | tf_op jit(solution)/shard_map/transpose(jvp())/while/body/eval_jaxpr/checkpoint/shp,shn->hpn/dot_general | solution.py:51
  403.6 11.9 %convolution_convert_fusion = bf16[256,4096]{1,0:T(8,128)(2,1)} fusion(bf16[256,2048]{1,0:T(8,128)(2,1)} %get-tuple-element.242, bf16[4096,2048]{1,0:T(8,128)(2,1)} %all-gather.3.cloned.1.call-done), kind=kOutput, calls=%fused_computation.20 | convolution fusion | flops 4296015872 | bytes 19922944 | tf_op jit(solution)/shard_map/dot_general | solution.py:128
  418.2 16.7 %fusion.40 = (f32[32,256]{1,0:T(8,128)S(1)}, f32[32,256]{1,0:T(8,128)S(1)}, f32[32,256,256]{2,1,0:T(8,128)S(1)}, f32[32,256,256]{2,1,0:T(8,128)}) fusion(f32[32,256]{1,0:T(8,128)S(1)} %copy_bitcast_fusion, f32[2,256,256]{2,1,0:T(8,128)S(1)} %fusion.78, pred[256,256]{1,0:T(8,128)(4,1)S(1)} %compare_and_fusion, f32[256,32,64]{0,2,1:T(8,128)} %squeeze.60, ...), kind=kOutput, calls=%fused_computation.66 | convolution fusion | flops 1639956480 | bytes 21659648 | tf_op jit(solution)/shard_map/transpose(jvp())/while/body/eval_jaxpr/checkpoint/hts,shp->thp/dot_general | solution.py:42
  441.7 6.6 %bitcast_add_fusion = f32[256,32,64]{0,2,1:T(8,128)} fusion(f32[32,64,256]{2,1,0:T(8,128)S(1)} %copy-done.8, f32[32,256,256]{2,1,0:T(8,128)S(1)} %get-tuple-element.245, f32[256,32,64]{0,2,1:T(8,128)S(1)} %bitcast.239, f32[256,32]{0,1:T(8,128)S(1)} %get-tuple-element.247), kind=kOutput, calls=%fused_computation.39 | convolution fusion | flops 1611661312 | bytes 14712832 | tf_op jit(solution)/shard_map/transpose(jvp())/while/body/eval_jaxpr/checkpoint/hts,shp->thp/dot_general | solution.py:42
  462.9 8.4 %bitcast_reduce_fusion.1 = f32[256,2,128]{2,0,1:T(8,128)S(1)} fusion(f32[32,64,128]{2,1,0:T(8,128)} %copy-done, f32[256,32,64]{0,2,1:T(8,128)S(1)} %bitcast.240, f32[256,32]{0,1:T(8,128)S(1)} %bitcast.267), kind=kOutput, calls=%fused_computation.21 | convolution fusion | flops 806813696 | bytes 3440640 | tf_op jit(solution)/shard_map/transpose(jvp(thn,hpn->thp))/dot_general | solution.py:83
  472.1 9.1 %bitcast_reduce_fusion.2 = f32[256,2,128]{2,0,1:T(8,128)} fusion(f32[32,64,128]{2,1,0:T(8,128)} %copy-done.5, f32[256,32,64]{0,2,1:T(8,128)S(1)} %bitcast.241, f32[256,32]{0,1:T(8,128)S(1)} %copy-done.23), kind=kOutput, calls=%fused_computation.22 | convolution fusion | flops 806813696 | bytes 3440640 | tf_op jit(solution)/shard_map/transpose(jvp())/while/body/eval_jaxpr/checkpoint/thn,hpn->thp/dot_general | solution.py:47
  (239 shorter events, 173.0 us)
Async XLA Ops:
  7.2 169.8 %all-gather.5.cloned.1.call-start = ((), (), s32[]{:S(2)}) async-start(), calls=%async_computation.4 | async-start | bytes 2621440 | tf_op jit(solution)/shard_map/all_gather | solution.py:134
  7.9 169.1 %all-gather.3.cloned.1.call-start = ((), (), s32[]{:S(2)}) async-start(), calls=%async_computation.2 | async-start | bytes 18874368 | tf_op jit(solution)/shard_map/all_gather | solution.py:127
  8.7 488.5 %reduce-scatter.5.cloned.1.call-start = ((), (), s32[]{:S(2)}) async-start(), calls=%async_computation.5 | async-start | bytes 18874368 | tf_op jit(solution)/shard_map/reduce_scatter | solution.py:136
  10.9 9.7 %copy-start.34 = (f32[256]{0:T(256)}, f32[256]{0:T(256)S(1)}, u32[]{:S(2)}) copy-start(f32[256]{0:T(256)S(1)} %get-tuple-element.238) | copy-start | bytes 3076
  11.6 9.3 %copy-start.41 = (f32[32]{0:T(128)}, f32[32]{0:T(128)S(1)}, u32[]{:S(2)}) copy-start(f32[32]{0:T(128)S(1)} %reduce_sum.186) | copy-start | bytes 388
  12.2 8.4 %copy-start.14 = (f32[32,2,128]{2,0,1:T(8,128)}, f32[32,2,128]{2,0,1:T(8,128)S(1)}, u32[]{:S(2)}) copy-start(f32[32,2,128]{2,0,1:T(8,128)S(1)} %reduce-window.55) | copy-start | bytes 98308
  12.4 8.2 %copy-start.28 = (f32[32,2]{0,1:T(2,128)}, f32[32,2]{0,1:T(2,128)S(1)}, u32[]{:S(2)}) copy-start(f32[32,2]{0,1:T(2,128)S(1)} %slice.68) | copy-start | bytes 772
  20.7 148.2 %copy-start.16 = (f32[32,256]{1,0:T(8,128)}, f32[32,256]{1,0:T(8,128)S(1)}, u32[]{:S(2)}) copy-start(f32[32,256]{1,0:T(8,128)S(1)} %get-tuple-element.249) | copy-start | bytes 98308
  25.4 10.1 %collective-permute-start = (bf16[32,64,128]{2,1,0:T(8,128)(2,1)}, bf16[32,64,128]{2,1,0:T(8,128)(2,1)}, u32[]{:S(2)}, u32[]{:S(2)}) collective-permute-start(bf16[32,64,128]{2,1,0:T(8,128)(2,1)} %fusion.114), channel_id=1, source_target_pairs={{0,4},{4,8},{8,12},{12,16},{16,20},{20,24},{24,28},{1,5},{5,9},{9,... | collective-permute-start | bytes 1572872 | tf_op jit(solution)/shard_map/while/body/eval_jaxpr/ppermute | solution.py:16
  37.7 11.7 %collective-permute-start = (bf16[32,64,128]{2,1,0:T(8,128)(2,1)}, bf16[32,64,128]{2,1,0:T(8,128)(2,1)}, u32[]{:S(2)}, u32[]{:S(2)}) collective-permute-start(bf16[32,64,128]{2,1,0:T(8,128)(2,1)} %fusion.114), channel_id=1, source_target_pairs={{0,4},{4,8},{8,12},{12,16},{16,20},{20,24},{24,28},{1,5},{5,9},{9,... | collective-permute-start | bytes 1572872 | tf_op jit(solution)/shard_map/while/body/eval_jaxpr/ppermute | solution.py:16
  51.5 11.7 %collective-permute-start = (bf16[32,64,128]{2,1,0:T(8,128)(2,1)}, bf16[32,64,128]{2,1,0:T(8,128)(2,1)}, u32[]{:S(2)}, u32[]{:S(2)}) collective-permute-start(bf16[32,64,128]{2,1,0:T(8,128)(2,1)} %fusion.114), channel_id=1, source_target_pairs={{0,4},{4,8},{8,12},{12,16},{16,20},{20,24},{24,28},{1,5},{5,9},{9,... | collective-permute-start | bytes 1572872 | tf_op jit(solution)/shard_map/while/body/eval_jaxpr/ppermute | solution.py:16
  65.4 23.0 %collective-permute-start = (bf16[32,64,128]{2,1,0:T(8,128)(2,1)}, bf16[32,64,128]{2,1,0:T(8,128)(2,1)}, u32[]{:S(2)}, u32[]{:S(2)}) collective-permute-start(bf16[32,64,128]{2,1,0:T(8,128)(2,1)} %fusion.114), channel_id=1, source_target_pairs={{0,4},{4,8},{8,12},{12,16},{16,20},{20,24},{24,28},{1,5},{5,9},{9,... | collective-permute-start | bytes 1572872 | tf_op jit(solution)/shard_map/while/body/eval_jaxpr/ppermute | solution.py:16
  90.6 11.7 %collective-permute-start = (bf16[32,64,128]{2,1,0:T(8,128)(2,1)}, bf16[32,64,128]{2,1,0:T(8,128)(2,1)}, u32[]{:S(2)}, u32[]{:S(2)}) collective-permute-start(bf16[32,64,128]{2,1,0:T(8,128)(2,1)} %fusion.114), channel_id=1, source_target_pairs={{0,4},{4,8},{8,12},{12,16},{16,20},{20,24},{24,28},{1,5},{5,9},{9,... | collective-permute-start | bytes 1572872 | tf_op jit(solution)/shard_map/while/body/eval_jaxpr/ppermute | solution.py:16
  104.5 23.1 %collective-permute-start = (bf16[32,64,128]{2,1,0:T(8,128)(2,1)}, bf16[32,64,128]{2,1,0:T(8,128)(2,1)}, u32[]{:S(2)}, u32[]{:S(2)}) collective-permute-start(bf16[32,64,128]{2,1,0:T(8,128)(2,1)} %fusion.114), channel_id=1, source_target_pairs={{0,4},{4,8},{8,12},{12,16},{16,20},{20,24},{24,28},{1,5},{5,9},{9,... | collective-permute-start | bytes 1572872 | tf_op jit(solution)/shard_map/while/body/eval_jaxpr/ppermute | solution.py:16
  129.7 22.9 %collective-permute-start = (bf16[32,64,128]{2,1,0:T(8,128)(2,1)}, bf16[32,64,128]{2,1,0:T(8,128)(2,1)}, u32[]{:S(2)}, u32[]{:S(2)}) collective-permute-start(bf16[32,64,128]{2,1,0:T(8,128)(2,1)} %fusion.114), channel_id=1, source_target_pairs={{0,4},{4,8},{8,12},{12,16},{16,20},{20,24},{24,28},{1,5},{5,9},{9,... | collective-permute-start | bytes 1572872 | tf_op jit(solution)/shard_map/while/body/eval_jaxpr/ppermute | solution.py:16
  155.6 13.3 %copy-start.1 = (f32[256,2,16,128]{3,0,2,1:T(8,128)}, f32[256,2,16,128]{3,0,2,1:T(8,128)S(1)}, u32[]{:S(2)}) copy-start(f32[256,2,16,128]{3,0,2,1:T(8,128)S(1)} %broadcast_in_dim.135) | copy-start | bytes 12582916
  160.2 8.6 %copy-start.4 = (f32[32,64,256]{2,1,0:T(8,128)}, f32[32,64,256]{2,1,0:T(8,128)S(1)}, u32[]{:S(2)}) copy-start(f32[32,64,256]{2,1,0:T(8,128)S(1)} %fusion.77) | copy-start | bytes 6291460
  229.7 271.5 %reduce-scatter.3.cloned.1.call-start = ((), (), s32[]{:S(2)}) async-start(), calls=%async_computation.3 | async-start | bytes 2621440 | tf_op jit(solution)/shard_map/reduce_scatter | solution.py:131
  240.9 147.7 %copy-start.22 = (f32[32,256]{1,0:T(8,128)S(1)}, f32[32,256]{1,0:T(8,128)}, u32[]{:S(2)}) copy-start(f32[32,256]{1,0:T(8,128)} %param.17) | copy-start | bytes 98308
  243.3 13.0 %collective-permute-start.1 = (bf16[32,64,128]{2,1,0:T(8,128)(2,1)}, bf16[32,64,128]{2,1,0:T(8,128)(2,1)}, u32[]{:S(2)}, u32[]{:S(2)}) collective-permute-start(bf16[32,64,128]{2,1,0:T(8,128)(2,1)} %fusion.115), channel_id=1, source_target_pairs={{4,0},{8,4},{12,8},{16,12},{20,16},{24,20},{28,24},{5,1},{9,5},{13... | collective-permute-start | bytes 1572872 | tf_op jit(solution)/shard_map/while/body/eval_jaxpr/ppermute | solution.py:16
  260.0 14.9 %collective-permute-start.1 = (bf16[32,64,128]{2,1,0:T(8,128)(2,1)}, bf16[32,64,128]{2,1,0:T(8,128)(2,1)}, u32[]{:S(2)}, u32[]{:S(2)}) collective-permute-start(bf16[32,64,128]{2,1,0:T(8,128)(2,1)} %fusion.115), channel_id=1, source_target_pairs={{4,0},{8,4},{12,8},{16,12},{20,16},{24,20},{28,24},{5,1},{9,5},{13... | collective-permute-start | bytes 1572872 | tf_op jit(solution)/shard_map/while/body/eval_jaxpr/ppermute | solution.py:16
  278.4 22.9 %collective-permute-start.1 = (bf16[32,64,128]{2,1,0:T(8,128)(2,1)}, bf16[32,64,128]{2,1,0:T(8,128)(2,1)}, u32[]{:S(2)}, u32[]{:S(2)}) collective-permute-start(bf16[32,64,128]{2,1,0:T(8,128)(2,1)} %fusion.115), channel_id=1, source_target_pairs={{4,0},{8,4},{12,8},{16,12},{20,16},{24,20},{28,24},{5,1},{9,5},{13... | collective-permute-start | bytes 1572872 | tf_op jit(solution)/shard_map/while/body/eval_jaxpr/ppermute | solution.py:16
  304.7 22.9 %collective-permute-start.1 = (bf16[32,64,128]{2,1,0:T(8,128)(2,1)}, bf16[32,64,128]{2,1,0:T(8,128)(2,1)}, u32[]{:S(2)}, u32[]{:S(2)}) collective-permute-start(bf16[32,64,128]{2,1,0:T(8,128)(2,1)} %fusion.115), channel_id=1, source_target_pairs={{4,0},{8,4},{12,8},{16,12},{20,16},{24,20},{28,24},{5,1},{9,5},{13... | collective-permute-start | bytes 1572872 | tf_op jit(solution)/shard_map/while/body/eval_jaxpr/ppermute | solution.py:16
  331.0 22.7 %collective-permute-start.1 = (bf16[32,64,128]{2,1,0:T(8,128)(2,1)}, bf16[32,64,128]{2,1,0:T(8,128)(2,1)}, u32[]{:S(2)}, u32[]{:S(2)}) collective-permute-start(bf16[32,64,128]{2,1,0:T(8,128)(2,1)} %fusion.115), channel_id=1, source_target_pairs={{4,0},{8,4},{12,8},{16,12},{20,16},{24,20},{28,24},{5,1},{9,5},{13... | collective-permute-start | bytes 1572872 | tf_op jit(solution)/shard_map/while/body/eval_jaxpr/ppermute | solution.py:16
  357.1 13.4 %collective-permute-start.1 = (bf16[32,64,128]{2,1,0:T(8,128)(2,1)}, bf16[32,64,128]{2,1,0:T(8,128)(2,1)}, u32[]{:S(2)}, u32[]{:S(2)}) collective-permute-start(bf16[32,64,128]{2,1,0:T(8,128)(2,1)} %fusion.115), channel_id=1, source_target_pairs={{4,0},{8,4},{12,8},{16,12},{20,16},{24,20},{28,24},{5,1},{9,5},{13... | collective-permute-start | bytes 1572872 | tf_op jit(solution)/shard_map/while/body/eval_jaxpr/ppermute | solution.py:16
  373.9 11.7 %collective-permute-start.1 = (bf16[32,64,128]{2,1,0:T(8,128)(2,1)}, bf16[32,64,128]{2,1,0:T(8,128)(2,1)}, u32[]{:S(2)}, u32[]{:S(2)}) collective-permute-start(bf16[32,64,128]{2,1,0:T(8,128)(2,1)} %fusion.115), channel_id=1, source_target_pairs={{4,0},{8,4},{12,8},{16,12},{20,16},{24,20},{28,24},{5,1},{9,5},{13... | collective-permute-start | bytes 1572872 | tf_op jit(solution)/shard_map/while/body/eval_jaxpr/ppermute | solution.py:16
  389.4 12.8 %copy-start.30 = (f32[32,2]{0,1:T(2,128)}, f32[32,2]{0,1:T(2,128)S(1)}, u32[]{:S(2)}) copy-start(f32[32,2]{0,1:T(2,128)S(1)} %slice.73) | copy-start | bytes 772
  393.8 8.3 %copy-start.38 = (f32[32]{0:T(128)}, f32[32]{0:T(128)S(1)}, u32[]{:S(2)}) copy-start(f32[32]{0:T(128)S(1)} %slice_reduce_fusion.4) | copy-start | bytes 388
  416.6 18.3 %copy-start.18 = (pred[256,256]{1,0:T(8,128)(4,1)}, pred[256,256]{1,0:T(8,128)(4,1)S(1)}, u32[]{:S(2)}) copy-start(pred[256,256]{1,0:T(8,128)(4,1)S(1)} %compare_and_fusion) | copy-start | bytes 196612
  418.2 16.7 %copy-start.13 = (f32[256,2,128]{2,0,1:T(8,128)S(1)}, f32[256,2,128]{2,0,1:T(8,128)}, u32[]{:S(2)}) copy-start(f32[256,2,128]{2,0,1:T(8,128)} %copy.185) | copy-start | bytes 786436
  462.9 9.2 %copy-start.23 = (f32[256,32]{0,1:T(8,128)S(1)}, f32[256,32]{0,1:T(8,128)}, u32[]{:S(2)}) copy-start(f32[256,32]{0,1:T(8,128)} %get-tuple-element.248) | copy-start | bytes 98308
  472.1 10.9 %copy-start.10 = (f32[256,2,128]{0,2,1:T(8,128)S(1)}, f32[256,2,128]{0,2,1:T(8,128)}, u32[]{:S(2)}) copy-start(f32[256,2,128]{0,2,1:T(8,128)} %squeeze.62) | copy-start | bytes 786436
  (29 other events, 100.1 us)
Sparse Core Ops, SparseCore 0:
  9.6 45.2 all-gather.4
  56.7 106.9 all-gather.2
  229.8 137.1 reduce-scatter.4
  415.7 40.9 reduce-scatter.2
where the time goes:
time: 515 us; the launch traced here: 508 us
  waiting for transfers between devices  188 us (37%)
  matrix products  128 us (25%)
  other arithmetic  77.4 us (15%)
  local copies, waits for them, and re-layouts  49.7 us (10%)
  starting transfers between devices  49.1 us (10%)
  between operations  15.4 us (3%)
    ppermute x14, waiting for transfers between devices, from_behind(): lax.ppermute(value, axis, [(source, source + steps) for source in range(l...  187 us
    ppermute x14, starting transfers between devices, from_behind(): lax.ppermute(value, axis, [(source, source + steps) for source in range(l...  49 us
    dot_general x3, matrix products, advance(): jnp.einsum('hts,shp->thp', scores, x_here, precision=lax.Precision.HIGHEST)  31.9 us
    dot_general x3, matrix products, advance(): jnp.einsum('thn,hpn->thp', c_heads, state, precision=lax.Precision.HIGHEST)  19.7 us
    unnamed x93, local copies, waits for them, and re-layouts  19.1 us
    dot_general x3, matrix products, carried_term(): jnp.einsum('thn,hpn->thp', c_heads, state, precision=lax.Precision.HIGHEST)  19.1 us
    convert_element_type x7, other arithmetic, backward_step(): (g_local[:, None, None] * carried + adjoint_in).astype(jnp.bfloat16)  15.9 us
    dot_general x1, matrix products, per_device(): grad_y = jnp.dot(grad_full, full_weight, preferred_element_type=jnp.float32)  14.1 us
  transfers between devices with their start and end apart: 18, of which 14 were waited for; matrix products, arithmetic and copies ran while one was open for 39% of the time, Pallas kernels for 0%

commit v1 on v0

v1 whole, which is shorter than its diff:
```python
import jax
import jax.numpy as jnp
from jax import lax
from jax.experimental import pallas as pl
from jax.experimental.pallas import tpu as pltpu
from jax.sharding import PartitionSpec as P

P_SIZE = 64
N = 128
GROUP = 1024
HEADS = GROUP // P_SIZE
ROWS = HEADS + 8
F32 = jnp.float32
BF16 = jnp.bfloat16
NN = (((1,), (0,)), ((), ()))
NT = (((1,), (1,)), ((), ()))
TN = (((0,), (0,)), ((), ()))


def mm(a, b, dims=NN):
    return lax.dot_general(a, b, dims, preferred_element_type=F32)


def exact(a, b, dims=NN):
    return lax.dot_general(
        a, b, dims, preferred_element_type=F32, precision=lax.Precision.HIGHEST
    )


def grid_order(tokens):
    row = lax.broadcasted_iota(jnp.int32, (tokens, tokens), 0)
    col = lax.broadcasted_iota(jnp.int32, (tokens, tokens), 1)
    return row, col


def segments():
    head = lax.broadcasted_iota(jnp.int32, (HEADS, GROUP), 0)
    lane = lax.broadcasted_iota(jnp.int32, (HEADS, GROUP), 1)
    return jnp.where(lane // P_SIZE == head, 1.0, 0.0).astype(BF16)


def entry_of(cum_t):
    keep = cum_t[:, HEADS : HEADS + 1] < 0.5
    entry = jnp.where(keep, jnp.exp(cum_t[:, :HEADS]), 0.0)
    return mm(entry.astype(BF16), segments())


def tail_of(cum_t):
    last = cum_t[-1:, :]
    keep = cum_t[:, HEADS : HEADS + 1] == last[:, HEADS : HEADS + 1]
    tail = jnp.where(keep, jnp.exp(last[:, :HEADS] - cum_t[:, :HEADS]), 0.0)
    return mm(tail.astype(BF16), segments())


def local_state_kernel(decay_ref, x_ref, b_ref, state_ref, cum_ref, cum_t_ref):
    tokens = x_ref.shape[0]
    row, col = grid_order(tokens)
    decay = decay_ref[...]
    cum_ref[...] = exact(decay, jnp.where(row <= col, 1.0, 0.0))
    cum_t = exact(jnp.where(col <= row, 1.0, 0.0), decay, NT)
    cum_t_ref[...] = cum_t
    weighted = (x_ref[...].astype(F32) * tail_of(cum_t)).astype(BF16)
    state_ref[...] = mm(b_ref[...], weighted, TN).astype(BF16)


def forward_kernel(
    x_ref, b_ref, c_ref, z_ref, cum_ref, cum_t_ref, state_ref, gain_ref, y_ref, normed_ref
):
    tokens = x_ref.shape[0]
    row, col = grid_order(tokens)
    cum = cum_ref[...]
    cum_t = cum_t_ref[...]
    same = (col <= row) & (cum_t[:, HEADS : HEADS + 1] == cum[HEADS : HEADS + 1, :])
    scores = mm(c_ref[...], b_ref[...], NT)
    y_ref[...] = mm(c_ref[...], state_ref[...]) * entry_of(cum_t)
    low = lax.broadcasted_iota(jnp.int32, (tokens, 2 * P_SIZE), 1) < P_SIZE
    zero = jnp.zeros((tokens, 2 * P_SIZE), BF16)

    def weights(head):
        spread = cum_t[:, head : head + 1] - cum[head : head + 1, :]
        return (jnp.exp(jnp.where(same, spread, -1e30)) * scores).astype(BF16)

    for pair in range(HEADS // 2):
        lanes = slice(pair * 2 * P_SIZE, (pair + 1) * 2 * P_SIZE)
        x_pair = x_ref[:, lanes]
        y_ref[:, lanes] += mm(weights(2 * pair), jnp.where(low, x_pair, zero)) + mm(
            weights(2 * pair + 1), jnp.where(low, zero, x_pair)
        )
    z = z_ref[...].astype(F32)
    gated = y_ref[...] * (z / (1.0 + jnp.exp(-z)))
    scale = lax.rsqrt(jnp.mean(gated * gated, axis=1, keepdims=True) + 1e-05)
    normed_ref[...] = (gated * scale * gain_ref[...]).astype(BF16)


def norm_grad_kernel(
    y_ref, z_ref, gain_ref, grad_ref, c_ref, cum_t_ref, dy_ref, dz_ref, adjoint_ref
):
    z = z_ref[...].astype(F32)
    y = y_ref[...]
    sig = 1.0 / (1.0 + jnp.exp(-z))
    silu = z * sig
    gated = y * silu
    scale = lax.rsqrt(jnp.mean(gated * gated, axis=1, keepdims=True) + 1e-05)
    up = grad_ref[...].astype(F32) * gain_ref[...]
    shared = jnp.mean(up * gated, axis=1, keepdims=True)
    d_gated = scale * (up - gated * (scale * scale * shared))
    dz_ref[...] = d_gated * y * (sig * (1.0 + z * (1.0 - sig)))
    dy = d_gated * silu
    dy_ref[...] = dy.astype(BF16)
    adjoint_ref[...] = mm(
        c_ref[...], (dy * entry_of(cum_t_ref[...])).astype(BF16), TN
    ).astype(BF16)


def scan_grad_kernel(
    x_ref, b_ref, c_ref, dy_ref, cum_ref, cum_t_ref, state_ref, adjoint_ref,
    dx_ref, db_ref, dc_ref, decay_ref,
):
    tokens = x_ref.shape[0]
    row, col = grid_order(tokens)
    cum = cum_ref[...]
    cum_t = cum_t_ref[...]
    b = b_ref[...]
    c = c_ref[...]
    segment = segments()
    state = state_ref[...]
    adjoint = adjoint_ref[...]
    same = (row <= col) & (cum_t[:, HEADS : HEADS + 1] == cum[HEADS : HEADS + 1, :])
    scores = mm(b, c, NT)
    after = jnp.where(row >= col, 1.0, 0.0)
    after_bf = after.astype(BF16)
    before = row < col
    low = lax.broadcasted_iota(jnp.int32, (tokens, 2 * P_SIZE), 1) < P_SIZE
    zero = jnp.zeros((tokens, 2 * P_SIZE), BF16)

    tail = tail_of(cum_t)
    tail_x = x_ref[...].astype(F32) * tail
    back = mm(b, adjoint)
    dx_ref[...] = back * tail
    tail_sum = mm(segment, (tail_x * back).astype(BF16), NT)
    db_tail = mm(tail_x.astype(BF16), adjoint, NT)
    entry_dy = dy_ref[...].astype(F32) * entry_of(cum_t)
    entry_sum = mm(segment, (entry_dy * mm(c, state)).astype(BF16), NT)
    dc_entry = mm(entry_dy.astype(BF16), state, NT)
    through = mm(segment, (adjoint.astype(F32) * state.astype(F32)).astype(BF16), NT)
    through = jnp.sum(through, axis=1, keepdims=True)
    whole = jnp.where(
        cum[HEADS : HEADS + 1, -1:] < 0.5, jnp.exp(cum[:HEADS, -1:]), 0.0
    )
    decay_ref[...] = (
        exact(entry_sum, after) + exact(tail_sum, 1.0 - after) + whole * through
    )

    d_scores = jnp.zeros((tokens, tokens), F32)
    for pair in range(HEADS // 2):
        lanes = slice(pair * 2 * P_SIZE, (pair + 1) * 2 * P_SIZE)
        x_pair = x_ref[:, lanes]
        dy_pair = dy_ref[:, lanes]
        add = jnp.zeros((tokens, 2 * P_SIZE), F32)
        for half in range(2):
            head = 2 * pair + half
            dy_half = jnp.where(low, dy_pair, zero) if half == 0 else jnp.where(low, zero, dy_pair)
            spread = cum[head : head + 1, :] - cum_t[:, head : head + 1]
            weight = jnp.exp(jnp.where(same, spread, -1e30))
            weighted = weight * scores
            add += mm(weighted.astype(BF16), dy_half)
            d_weighted = mm(x_pair, dy_half, NT)
            d_scores += d_weighted * weight
            spans = mm((d_weighted * weighted).astype(BF16), after_bf)
            decay_ref[head : head + 1, :] += jnp.sum(
                jnp.where(before, spans, 0.0), axis=0, keepdims=True
            )
        dx_ref[:, lanes] += add
    d_scores = d_scores.astype(BF16)
    db_ref[...] = mm(d_scores, c) + db_tail
    dc_ref[...] = mm(d_scores, b, TN) + dc_entry


def group_specs(shapes):
    def spec(kind, tokens):
        if kind == "wide":
            return pl.BlockSpec((tokens, GROUP), lambda g: (0, g))
        if kind == "narrow":
            return pl.BlockSpec((tokens, N), lambda g: (0, g))
        if kind == "state":
            return pl.BlockSpec((N, GROUP), lambda g: (0, g))
        if kind == "gain":
            return pl.BlockSpec((1, GROUP), lambda g: (0, g))
        if kind == "rows":
            return pl.BlockSpec((None, ROWS, tokens), lambda g: (g, 0, 0))
        if kind == "columns":
            return pl.BlockSpec((None, tokens, ROWS), lambda g: (g, 0, 0))
        return pl.BlockSpec((HEADS, tokens), lambda g: (g, 0))

    return [spec(kind, tokens) for kind, tokens in shapes]


def run(kernel, groups, tokens, in_kinds, out_kinds, dtypes, flops, *args):
    shape = {
        "wide": (tokens, groups * GROUP),
        "narrow": (tokens, groups * N),
        "state": (N, groups * GROUP),
        "rows": (groups, ROWS, tokens),
        "columns": (groups, tokens, ROWS),
        "heads": (groups * HEADS, tokens),
    }
    return pl.pallas_call(
        kernel,
        grid=(groups,),
        in_specs=group_specs([(k, tokens) for k in in_kinds]),
        out_specs=group_specs([(k, tokens) for k in out_kinds]),
        out_shape=[jax.ShapeDtypeStruct(shape[k], d) for k, d in zip(out_kinds, dtypes)],
        cost_estimate=pl.CostEstimate(
            flops=flops * groups, bytes_accessed=4 * tokens * GROUP * groups * 4,
            transcendentals=tokens * tokens * HEADS * groups,
        ),
        compiler_params=pltpu.CompilerParams(vmem_limit_bytes=48 << 20),
    )(*args)


def pass_states(local, decays, reverse):
    count = lax.axis_size("seq")
    slices = lax.all_to_all(local, "seq", 0, 0, tiled=True)
    slices = slices.reshape(count, N // count, -1).astype(F32)
    factor = jnp.repeat(decays, P_SIZE, axis=1)
    carried = jnp.zeros(slices.shape[1:], F32)
    incoming = [None] * count
    for step in range(count):
        here = count - 1 - step if reverse else step
        incoming[here] = carried.astype(BF16)
        carried = factor[here][None, :] * carried + slices[here]
    return lax.all_to_all(jnp.concatenate(incoming, axis=0), "seq", 0, 0, tiled=True)


def per_device(
    inputs_x, inputs_b, inputs_c, gate_z, log_decay, resets, norm_gain, out_weight, out_grad
):
    tokens, width = inputs_x.shape
    groups = width // GROUP
    square = 2 * tokens * tokens * GROUP
    gain = norm_gain[None, :]

    full_weight = lax.all_gather(out_weight, "seq", axis=0, tiled=True)
    grad_full = lax.all_gather(out_grad, "head", axis=1, tiled=True)
    whole = jnp.exp(jnp.sum(log_decay, axis=1)) * (jnp.sum(resets) == 0).astype(F32)
    decays = lax.all_gather(whole, "seq", axis=0)

    decay_rows = jnp.concatenate(
        [
            log_decay.reshape(groups, HEADS, tokens),
            jnp.broadcast_to(resets.astype(F32)[None, None, :], (groups, 8, tokens)),
        ],
        axis=1,
    )
    local, cum, cum_t = run(
        local_state_kernel, groups, tokens, ("rows", "wide", "narrow"),
        ("state", "rows", "columns"), (BF16, F32, F32), square,
        decay_rows, inputs_x, inputs_b,
    )
    state_in = pass_states(local, decays, False)
    y, normed_bf = run(
        forward_kernel, groups, tokens,
        ("wide", "narrow", "narrow", "wide", "rows", "columns", "state", "gain"),
        ("wide", "wide"), (F32, BF16), 3 * square,
        inputs_x, inputs_b, inputs_c, gate_z, cum, cum_t, state_in, gain,
    )
    grad_weight = lax.psum_scatter(
        mm(grad_full, normed_bf, TN).astype(BF16), "seq", scatter_dimension=0, tiled=True
    ).astype(F32)
    grad_y = mm(grad_full, full_weight)
    dy, grad_z, adjoint = run(
        norm_grad_kernel, groups, tokens,
        ("wide", "wide", "gain", "wide", "narrow", "columns"),
        ("wide", "wide", "state"), (BF16, F32, BF16), square,
        y, gate_z, gain, grad_y, inputs_c, cum_t,
    )
    layer_out = lax.psum_scatter(
        mm(normed_bf, full_weight, NT).astype(BF16), "head", scatter_dimension=1, tiled=True
    )
    adjoint_out = pass_states(adjoint, decays, True)
    grad_x, grad_b, grad_c, grad_decay = run(
        scan_grad_kernel, groups, tokens,
        ("wide", "narrow", "narrow", "wide", "rows", "columns", "state", "state"),
        ("wide", "narrow", "narrow", "heads"), (F32, F32, F32, F32), 10 * square,
        inputs_x, inputs_b, inputs_c, dy, cum, cum_t, state_in, adjoint_out,
    )
    return (layer_out, grad_x, grad_b, grad_c, grad_z, grad_decay, grad_weight)


def solution(mesh):
    wide = P("seq", "head")
    return jax.shard_map(
        per_device,
        mesh=mesh,
        in_specs=(wide, wide, wide, wide, P("head", "seq"), P("seq"), P("head"), wide, wide),
        out_specs=(wide, wide, wide, wide, wide, P("head", "seq"), wide),
        check_vma=False,
    )
```

time: 515 us -> 328 us (0.64)
  matrix products: 128 us -> 43 us
  other arithmetic: 77.4 us -> 5.69 us
  local copies, waits for them, and re-layouts: 49.7 us -> 12.2 us
  starting transfers between devices: 49.1 us -> 12.7 us
  blocking collectives: 0 us -> 25.2 us
  Pallas kernels: 0 us -> 21.6 us
    ppermute x14 -> x0, waiting for transfers between devices: 187 us -> none  [from_behind(): lax.ppermute(value, axis, [(source, source + steps) for source in range(l...]
    reduce_scatter x2, waiting for transfers between devices: 0.01 us -> 100 us  [the longest x1 70.9 us: per_device(): lax.psum_scatter(mm(grad_full, normed_bf, TN).astype(BF16), 'seq', scatte...]
    dot_general x19 -> x3, matrix products: 128 us -> 43 us  [mm(): return lax.dot_general(a, b, dims, preferred_element_type=F32)]
    all_gather x1, waiting for transfers between devices: 0.02 us -> 82.7 us  [per_device(): full_weight = lax.all_gather(out_weight, 'seq', axis=0, tiled=True)]
    ppermute x14 -> x0, starting transfers between devices: 49 us -> none  [from_behind(): lax.ppermute(value, axis, [(source, source + steps) for source in range(l...]
    convert_element_type x32 -> x2, other arithmetic: 41.1 us -> 0.2 us  [pass_states(): slices = slices.reshape(count, N // count, -1).astype(F32)]
    pallas_call x0 -> x4, Pallas kernels: none -> 21.6 us  [run(): pl.pallas_call(kernel, grid=(groups,), in_specs=group_specs([(k, tokens)...]
    reduce_sum x9 -> x2, other arithmetic: 14.1 us -> 0.74 us  [the longest x1 0.63 us: per_device(): jnp.sum(resets) == 0]
  transfers between devices with their start and end apart: 18 -> 7, of which waited for: 14 -> 4; matrix products, arithmetic and copies ran while one was open for 39% -> 17% of each run, Pallas kernels for 0% -> 7%
where the time goes in v1:
time: 328 us; the launch traced here: 323 us
  waiting for transfers between devices  187 us (57%)
  matrix products  43 us (13%)
  blocking collectives  25.2 us (8%)
  Pallas kernels  21.6 us (7%)
  between operations  15.4 us (5%)
  starting transfers between devices  12.7 us (4%)
  local copies, waits for them, and re-layouts  12.2 us (4%)
  other arithmetic  5.69 us (2%)
    all_gather x1, waiting for transfers between devices, per_device(): full_weight = lax.all_gather(out_weight, 'seq', axis=0, tiled=True)  82.7 us
    reduce_scatter x1, waiting for transfers between devices, per_device(): lax.psum_scatter(mm(grad_full, normed_bf, TN).astype(BF16), 'seq', scatte...  70.9 us
    dot_general x3, matrix products, mm(): return lax.dot_general(a, b, dims, preferred_element_type=F32)  43 us
    reduce_scatter x1, waiting for transfers between devices, per_device(): lax.psum_scatter(mm(normed_bf, full_weight, NT).astype(BF16), 'head', sca...  29.6 us
    pallas_call x4, Pallas kernels, run(): pl.pallas_call(kernel, grid=(groups,), in_specs=group_specs([(k, tokens)...  21.6 us
    all_to_all x1, blocking collectives, pass_states(): lax.all_to_all(jnp.concatenate(incoming, axis=0), 'seq', 0, 0, tiled=True)  13.3 us
    unnamed x1, blocking collectives  12 us
    unnamed x65, local copies, waits for them, and re-layouts  10.5 us
  transfers between devices with their start and end apart: 7, of which 4 were waited for; matrix products, arithmetic and copies ran while one was open for 17% of the time, Pallas kernels for 7%

profile of v1, /device:TPU:11, one launch (start us, length us, event | category | flops | bytes accessed | tf_op | source)
XLA Modules:
  0.0 323.1 jit_solution(8552191227828640597)
XLA Ops:
  7.3 0.7 all-gather.6.cloned.1.call-update
  8.0 0.7 all-gather.4.cloned.1.call-update
  8.7 0.6 fusion.28
  9.4 3.1 shard_map.144
  12.5 4.6 %all-to-all-start = ((bf16[8,16,2048]{2,1,0:T(8,128)(2,1)}), bf16[8,16,2048]{2,1,0:T(8,128)(2,1)S(1)}, u32[]{:S(2)}, u32[]{:S(2)}) async-start(bf16[8,16,2048]{2,1,0:T(8,128)(2,1)} %bitcast.2), calls=%async_computation | async-start | bytes 1048576 | tf_op jit(solution)/shard_map/all_to_all | solution.py:223
  19.2 12.0 %all-reduce = f32[256]{0:T(256)S(1)} all-reduce(f32[256]{0:T(256)S(1)} %multiply_dynamic-update-slice_fusion), channel_id=2, replica_groups=mesh['seq'=8,'head'=4] {'seq'}, use_global_device_ids=true, to_apply=%add | all-reduce | flops 256 | bytes 2048
  33.5 13.3 %all_to_all.40 = bf16[8,16,2048]{2,1,0:T(8,128)(2,1)S(1)} all-to-all(bf16[8,16,2048]{2,1,0:T(8,128)(2,1)S(1)} %bitcast.127), channel_id=1, replica_groups=mesh['seq'=8,'head'=4] {'seq'}, dimensions={0} | all-to-all | bytes 1048576 | tf_op jit(solution)/shard_map/all_to_all | solution.py:232
  46.8 4.7 %shard_map.145 = (f32[256,2048]{1,0:T(8,128)}, bf16[256,2048]{1,0:T(8,128)(2,1)S(1)}) custom-call(bf16[256,2048]{1,0:T(8,128)(2,1)S(1)} %copy-done.8, bf16[256,256]{1,0:T(8,128)(2,1)S(1)} %copy-done.12, bf16[256,256]{1,0:T(8,128)(2,1)S(1)} %copy-done.6, bf16[256,2048]{1,0:T(8,128)(2,1)S(1)} %copy-done.1, f32[2,24,256]{2,1,0:T(8,128)S(1)} %get-tuple-element.19.cum_ref, ...), custom_call_target="tpu_custom_call" | custom-call | flops 805306368 | bytes 8388608 | tf_op jit(solution)/shard_map/pallas_call | solution.py:207
  51.4 0.8 copy-done.3
  52.2 2.6 all-gather.6.cloned.1.call-done
  54.9 10.0 %convert_bitcast_fusion = bf16[4096,2048]{0,1:T(8,128)(2,1)} fusion(bf16[256,2048]{1,0:T(8,128)(2,1)S(1)} %get-tuple-element.22, bf16[256,4096]{1,0:T(8,128)(2,1)} %all-gather.6.cloned.1.call-done), kind=kOutput, calls=%fused_computation | convolution fusion | flops 4303355904 | bytes 19922944 | tf_op jit(solution)/shard_map/dot_general | solution.py:21
  64.9 82.7 %all-gather.4.cloned.1.call-done = bf16[4096,2048]{1,0:T(8,128)(2,1)} async-done(((bf16[512,2048]{1,0:T(8,128)(2,1)}), bf16[4096,2048]{1,0:T(8,128)(2,1)}) %all-gather.4.cloned.1.call-update) | async-done | bytes 16777232 | tf_op jit(solution)/shard_map/all_gather | solution.py:243
  147.6 12.3 %fusion.29.grad_ref = f32[256,2048]{1,0:T(8,128)} fusion(bf16[256,4096]{1,0:T(8,128)(2,1)} %all-gather.6.cloned.1.call-done, bf16[4096,2048]{1,0:T(8,128)(2,1)} %all-gather.4.cloned.1.call-done), kind=kOutput, calls=%fused_computation.55 | convolution fusion | flops 4294967296 | bytes 20971520 | tf_op jit(solution)/shard_map/dot_general | solution.py:21
  159.9 4.8 %shard_map.146 = (bf16[256,2048]{1,0:T(8,128)(2,1)S(1)}, f32[256,2048]{1,0:T(8,128)}, bf16[128,2048]{1,0:T(8,128)(2,1)S(1)}) custom-call(f32[256,2048]{1,0:T(8,128)S(1)} %copy-done, bf16[256,2048]{1,0:T(8,128)(2,1)S(1)} %copy-done.2, f32[1,2048]{1,0:T(1,128)S(1)} %bitcast.126, f32[256,2048]{1,0:T(8,128)} %fusion.29.grad_ref, bf16[256,256]{1,0:T(8,128)(2,1)S(1)} %copy-done.6, ...), custom_call_target="tpu_custom_call" | custom-call | flops 268435456 | bytes 8388608 | tf_op jit(solution)/shard_map/pallas_call | solution.py:207
  164.7 0.8 copy-done.5
  165.5 1.0 copy-done.10
  166.5 3.9 %all-to-all-start.2 = ((bf16[8,16,2048]{2,1,0:T(8,128)(2,1)}), bf16[8,16,2048]{2,1,0:T(8,128)(2,1)S(1)}, u32[]{:S(2)}, u32[]{:S(2)}) async-start(bf16[8,16,2048]{2,1,0:T(8,128)(2,1)} %bitcast.123), calls=%async_computation.3 | async-start | bytes 1048576 | tf_op jit(solution)/shard_map/all_to_all | solution.py:223
  170.4 20.8 %convolution_convert_fusion = bf16[256,4096]{1,0:T(8,128)(2,1)} fusion(bf16[256,2048]{1,0:T(8,128)(2,1)S(1)} %get-tuple-element.22, bf16[4096,2048]{1,0:T(8,128)(2,1)} %all-gather.4.cloned.1.call-done), kind=kOutput, calls=%fused_computation.1 | convolution fusion | flops 4296015872 | bytes 19922944 | tf_op jit(solution)/shard_map/dot_general | solution.py:21
  192.1 0.7 fusion.21
  193.4 0.6 convert_dynamic-update-slice_fusion.3
  194.0 0.6 convert_dynamic-update-slice_fusion.2
  194.7 0.6 convert_dynamic-update-slice_fusion.1
  195.3 0.6 convert_dynamic-update-slice_fusion
  195.9 0.6 fusion.18
  196.6 0.6 constant_dynamic-update-slice_fusion.1
  197.2 4.2 %all-to-all-start.3 = ((bf16[8,16,2048]{2,1,0:T(8,128)(2,1)}), bf16[8,16,2048]{2,1,0:T(8,128)(2,1)S(1)}, u32[]{:S(2)}, u32[]{:S(2)}) async-start(bf16[8,16,2048]{2,1,0:T(8,128)(2,1)} %bitcast.21), calls=%async_computation.4 | async-start | bytes 1048576 | tf_op jit(solution)/shard_map/all_to_all | solution.py:232
  201.4 70.9 %reduce-scatter.5.cloned.1.call-done = bf16[512,2048]{0,1:T(8,128)(2,1)} async-done(((bf16[4096,2048]{0,1:T(8,128)(2,1)}), bf16[512,2048]{0,1:T(8,128)(2,1)}) %reduce-scatter.5.cloned.1.call-update) | async-done | bytes 2097168 | tf_op jit(solution)/shard_map/reduce_scatter | solution.py:267
  272.3 4.1 %copy.16 = f32[512,2048]{1,0:T(8,128)} copy(bf16[512,2048]{0,1:T(8,128)(2,1)} %reduce-scatter.5.cloned.1.call-done) | data formatting | bytes 6291456
  276.4 0.9 copy-done.13
  277.3 0.8 copy-done.15
  278.1 8.9 %shard_map.147 = (f32[256,2048]{1,0:T(8,128)}, f32[256,256]{1,0:T(8,128)}, f32[256,256]{1,0:T(8,128)}, f32[32,256]{1,0:T(8,128)}) custom-call(bf16[256,2048]{1,0:T(8,128)(2,1)S(1)} %copy-done.9, bf16[256,256]{1,0:T(8,128)(2,1)S(1)} %copy-done.13, bf16[256,256]{1,0:T(8,128)(2,1)S(1)} %copy-done.6, bf16[256,2048]{1,0:T(8,128)(2,1)S(1)} %copy-done.11, ...), custom_call_target="tpu_custom_call" | custom-call | flops 2684354560 | bytes 8388608 | tf_op jit(solution)/shard_map/pallas_call | solution.py:207
  287.0 29.6 %reduce-scatter.3.cloned.1.call-done = bf16[256,1024]{1,0:T(8,128)(2,1)} async-done(((bf16[256,4096]{1,0:T(8,128)(2,1)}), bf16[256,1024]{1,0:T(8,128)(2,1)}) %reduce-scatter.3.cloned.1.call-update) | async-done | bytes 524304 | tf_op jit(solution)/shard_map/reduce_scatter | solution.py:277
  (98 shorter events, 4.6 us)
Async XLA Ops:
  7.2 1.5 copy-start.28
  7.2 2.2 copy-start.22
  7.2 2.2 copy-start.8
  7.2 2.2 copy-start.12
  7.2 47.7 %all-gather.6.cloned.1.call-start = ((), (), s32[]{:S(2)}) async-start(), calls=%async_computation.8 | async-start | bytes 2621440 | tf_op jit(solution)/shard_map/all_gather | solution.py:244
  7.9 139.7 %all-gather.4.cloned.1.call-start = ((), (), s32[]{:S(2)}) async-start(), calls=%async_computation.6 | async-start | bytes 18874368 | tf_op jit(solution)/shard_map/all_gather | solution.py:243
  9.4 8.5 %copy-start.29 = (u32[32]{0:T(128)S(1)}, u32[32]{0:T(128)}, u32[]{:S(2)}) copy-start(u32[32]{0:T(128)} %constant.9) | copy-start | bytes 388
  12.5 34.2 %copy-start.14 = (f32[2,24,256]{2,1,0:T(8,128)}, f32[2,24,256]{2,1,0:T(8,128)S(1)}, u32[]{:S(2)}) copy-start(f32[2,24,256]{2,1,0:T(8,128)S(1)} %get-tuple-element.19.cum_ref) | copy-start | bytes 147460
  12.5 20.3 %all-to-all-start = ((bf16[8,16,2048]{2,1,0:T(8,128)(2,1)}), bf16[8,16,2048]{2,1,0:T(8,128)(2,1)S(1)}, u32[]{:S(2)}, u32[]{:S(2)}) async-start(bf16[8,16,2048]{2,1,0:T(8,128)(2,1)} %bitcast.2), calls=%async_computation | async-start | bytes 1048576 | tf_op jit(solution)/shard_map/all_to_all | solution.py:223
  17.1 255.2 %reduce-scatter.5.cloned.1.call-start = ((), (), s32[]{:S(2)}) async-start(), calls=%async_computation.9 | async-start | bytes 18874368 | tf_op jit(solution)/shard_map/reduce_scatter | solution.py:267
  32.1 1.1 copy-start.23
  32.3 1.0 copy-start.18
  33.0 13.8 %copy-start.1 = (bf16[256,2048]{1,0:T(8,128)(2,1)S(1)}, bf16[256,2048]{1,0:T(8,128)(2,1)}, u32[]{:S(2)}) copy-start(bf16[256,2048]{1,0:T(8,128)(2,1)} %z_ref.3) | copy-start | bytes 3145732
  33.0 13.7 %copy-start.6 = (bf16[256,256]{1,0:T(8,128)(2,1)S(1)}, bf16[256,256]{1,0:T(8,128)(2,1)}, u32[]{:S(2)}) copy-start(bf16[256,256]{1,0:T(8,128)(2,1)} %c_ref.5) | copy-start | bytes 393220
  33.0 13.7 %copy-start.7 = (f32[2048]{0:T(1024)S(1)}, f32[2048]{0:T(1024)}, u32[]{:S(2)}) copy-start(f32[2048]{0:T(1024)} %param.15) | copy-start | bytes 24580
  51.4 0.8 copy-start.3
  64.9 95.0 %copy-start = (f32[256,2048]{1,0:T(8,128)S(1)}, f32[256,2048]{1,0:T(8,128)}, u32[]{:S(2)}) copy-start(f32[256,2048]{1,0:T(8,128)} %get-tuple-element.23.y_ref) | copy-start | bytes 6291460
  147.6 12.3 %copy-start.2 = (bf16[256,2048]{1,0:T(8,128)(2,1)S(1)}, bf16[256,2048]{1,0:T(8,128)(2,1)}, u32[]{:S(2)}) copy-start(bf16[256,2048]{1,0:T(8,128)(2,1)} %z_ref.3) | copy-start | bytes 3145732
  165.5 1.0 copy-start.10
  166.5 25.4 %all-to-all-start.2 = ((bf16[8,16,2048]{2,1,0:T(8,128)(2,1)}), bf16[8,16,2048]{2,1,0:T(8,128)(2,1)S(1)}, u32[]{:S(2)}, u32[]{:S(2)}) async-start(bf16[8,16,2048]{2,1,0:T(8,128)(2,1)} %bitcast.123), calls=%async_computation.3 | async-start | bytes 1048576 | tf_op jit(solution)/shard_map/all_to_all | solution.py:223
  170.4 146.2 %reduce-scatter.3.cloned.1.call-start = ((), (), s32[]{:S(2)}) async-start(), calls=%async_computation.7 | async-start | bytes 2621440 | tf_op jit(solution)/shard_map/reduce_scatter | solution.py:277
  191.2 0.9 copy-start.17
  191.2 0.9 copy-start.19
  191.2 0.9 copy-start.21
  191.2 0.9 copy-start.24
  191.2 0.9 copy-start.26
  197.2 79.2 %all-to-all-start.3 = ((bf16[8,16,2048]{2,1,0:T(8,128)(2,1)}), bf16[8,16,2048]{2,1,0:T(8,128)(2,1)S(1)}, u32[]{:S(2)}, u32[]{:S(2)}) async-start(bf16[8,16,2048]{2,1,0:T(8,128)(2,1)} %bitcast.21), calls=%async_computation.4 | async-start | bytes 1048576 | tf_op jit(solution)/shard_map/all_to_all | solution.py:232
  201.4 75.0 %copy-start.4 = (bf16[8,16,2048]{2,1,0:T(8,128)(2,1)S(1)}, bf16[8,16,2048]{2,1,0:T(8,128)(2,1)}, u32[]{:S(2)}) copy-start(bf16[8,16,2048]{2,1,0:T(8,128)(2,1)} %copy-done.3) | copy-start | bytes 1572868
  201.4 75.0 %copy-start.9 = (bf16[256,2048]{1,0:T(8,128)(2,1)S(1)}, bf16[256,2048]{1,0:T(8,128)(2,1)}, u32[]{:S(2)}) copy-start(bf16[256,2048]{1,0:T(8,128)(2,1)} %x_ref.5) | copy-start | bytes 3145732
  201.4 75.0 %copy-start.11 = (bf16[256,2048]{1,0:T(8,128)(2,1)S(1)}, bf16[256,2048]{1,0:T(8,128)(2,1)}, u32[]{:S(2)}) copy-start(bf16[256,2048]{1,0:T(8,128)(2,1)} %copy-done.10) | copy-start | bytes 3145732
  276.4 0.9 copy-start.13
  277.3 0.8 copy-start.15
  (5 other events, 3.3 us)
Sparse Core Ops, SparseCore 0:
  9.6 45.2 all-gather.5
  56.8 90.8 all-gather.3
  151.2 121.0 reduce-scatter.4
  275.0 41.5 reduce-scatter.2

commit v2 on v1

--- a/solution.py
+++ b/solution.py
@@ -232,6 +232,37 @@
     return lax.all_to_all(jnp.concatenate(incoming, axis=0), "seq", 0, 0, tiled=True)
 
 
+def shift(value, steps):
+    count = lax.axis_size("head")
+    return lax.ppermute(value, "head", [(i, (i + steps) % count) for i in range(count)])
+
+
+def gather_heads(value):
+    count = lax.axis_size("head")
+    width = value.shape[1]
+    me = lax.axis_index("head")
+    whole = jnp.zeros((value.shape[0], count * width), value.dtype)
+    for steps in range(count):
+        block = shift(value, steps) if steps else value
+        whole = lax.dynamic_update_slice(whole, block, (0, (me - steps) % count * width))
+    return whole
+
+
+def project(normed, weight):
+    count = lax.axis_size("head")
+    rows = weight.shape[0] // count
+    me = lax.axis_index("head")
+    total = None
+    for steps in list(range(1, count)) + [0]:
+        block = lax.dynamic_slice(
+            weight, ((me + steps) % count * rows, 0), (rows, weight.shape[1])
+        )
+        term = mm(normed, block, NT).astype(BF16)
+        term = (shift(term, steps) if steps else term).astype(F32)
+        total = term if total is None else total + term
+    return total.astype(BF16)
+
+
 def per_device(
     inputs_x, inputs_b, inputs_c, gate_z, log_decay, resets, norm_gain, out_weight, out_grad
 ):
@@ -241,9 +272,13 @@
     gain = norm_gain[None, :]
 
     full_weight = lax.all_gather(out_weight, "seq", axis=0, tiled=True)
-    grad_full = lax.all_gather(out_grad, "head", axis=1, tiled=True)
+    grad_full = gather_heads(out_grad)
+    grad_columns = lax.all_to_all(grad_full, "seq", 1, 0, tiled=True)
     whole = jnp.exp(jnp.sum(log_decay, axis=1)) * (jnp.sum(resets) == 0).astype(F32)
-    decays = lax.all_gather(whole, "seq", axis=0)
+    count = lax.axis_size("seq")
+    decays = lax.all_to_all(
+        jnp.broadcast_to(whole[None, :], (count, whole.shape[0])), "seq", 0, 0, tiled=True
+    )
 
     decay_rows = jnp.concatenate(
         [
@@ -264,9 +299,10 @@
         ("wide", "wide"), (F32, BF16), 3 * square,
         inputs_x, inputs_b, inputs_c, gate_z, cum, cum_t, state_in, gain,
     )
-    grad_weight = lax.psum_scatter(
-        mm(grad_full, normed_bf, TN).astype(BF16), "seq", scatter_dimension=0, tiled=True
-    ).astype(F32)
+    sent, full_weight, grad_columns = lax.optimization_barrier(
+        (normed_bf, full_weight, grad_columns)
+    )
+    normed_all = lax.all_gather(sent, "seq", axis=0, tiled=True)
     grad_y = mm(grad_full, full_weight)
     dy, grad_z, adjoint = run(
         norm_grad_kernel, groups, tokens,
@@ -274,9 +310,7 @@
         ("wide", "wide", "state"), (BF16, F32, BF16), square,
         y, gate_z, gain, grad_y, inputs_c, cum_t,
     )
-    layer_out = lax.psum_scatter(
-        mm(normed_bf, full_weight, NT).astype(BF16), "head", scatter_dimension=1, tiled=True
-    )
+    layer_out = project(normed_bf, full_weight)
     adjoint_out = pass_states(adjoint, decays, True)
     grad_x, grad_b, grad_c, grad_decay = run(
         scan_grad_kernel, groups, tokens,
@@ -284,6 +318,7 @@
         ("wide", "narrow", "narrow", "heads"), (F32, F32, F32, F32), 10 * square,
         inputs_x, inputs_b, inputs_c, dy, cum, cum_t, state_in, adjoint_out,
     )
+    grad_weight = mm(grad_columns, normed_all, TN)
     return (layer_out, grad_x, grad_b, grad_c, grad_z, grad_decay, grad_weight)
 
 

time: 328 us -> 241 us (0.73)
  waiting for transfers between devices: 187 us -> 93 us
  starting transfers between devices: 12.7 us -> 38.5 us
  blocking collectives: 25.2 us -> 0 us
  local copies, waits for them, and re-layouts: 12.2 us -> 16.9 us
  other arithmetic: 5.69 us -> 9.36 us
    reduce_scatter x2 -> x0, waiting for transfers between devices: 100 us -> none  [the longest x1 70.9 us: per_device(): lax.psum_scatter(mm(grad_full, normed_bf, TN).astype(BF16), 'seq', scatte...]
    all_gather x1, waiting for transfers between devices: 82.7 us -> 8.44 us  [per_device(): full_weight = lax.all_gather(out_weight, 'seq', axis=0, tiled=True)]
    all_to_all x0 -> x2, waiting for transfers between devices: none -> 40.7 us  [the longest x1 40.7 us: per_device(): grad_columns = lax.all_to_all(grad_full, 'seq', 1, 0, tiled=True)]
    ppermute x0 -> x6, waiting for transfers between devices: none -> 37 us  [shift(): lax.ppermute(value, 'head', [(i, (i + steps) % count) for i in range(coun...]
    all_to_all x1 -> x0, blocking collectives: 13.3 us -> none  [pass_states(): lax.all_to_all(jnp.concatenate(incoming, axis=0), 'seq', 0, 0, tiled=True)]
    unnamed x1 -> x0, blocking collectives: 12 us -> none
    all_to_all x0 -> x2, starting transfers between devices: none -> 9.41 us  [the longest x1 4.85 us: per_device(): grad_columns = lax.all_to_all(grad_full, 'seq', 1, 0, tiled=True)]
    all_to_all x1 -> x2, starting transfers between devices: 4.19 us -> 12.7 us  [pass_states(): lax.all_to_all(jnp.concatenate(incoming, axis=0), 'seq', 0, 0, tiled=True)]
  transfers between devices with their start and end apart: 7 -> 14, of which waited for: 4 -> 7; matrix products, arithmetic and copies ran while one was open for 17% -> 24% of each run, Pallas kernels for 7% -> 9%
where the time goes in v2:
time: 241 us; the launch traced here: 238 us
  waiting for transfers between devices  93 us (39%)
  matrix products  43.3 us (18%)
  starting transfers between devices  38.5 us (16%)
  Pallas kernels  21.7 us (9%)
  local copies, waits for them, and re-layouts  16.9 us (7%)
  between operations  14.9 us (6%)
  other arithmetic  9.36 us (4%)
    dot_general x6, matrix products, mm(): return lax.dot_general(a, b, dims, preferred_element_type=F32)  43.3 us
    all_to_all x1, waiting for transfers between devices, per_device(): grad_columns = lax.all_to_all(grad_full, 'seq', 1, 0, tiled=True)  40.7 us
    ppermute x6, waiting for transfers between devices, shift(): lax.ppermute(value, 'head', [(i, (i + steps) % count) for i in range(coun...  37 us
    pallas_call x4, Pallas kernels, run(): pl.pallas_call(kernel, grid=(groups,), in_specs=group_specs([(k, tokens)...  21.7 us
    all_to_all x2, starting transfers between devices, pass_states(): lax.all_to_all(jnp.concatenate(incoming, axis=0), 'seq', 0, 0, tiled=True)  12.7 us
    all_to_all x2, starting transfers between devices, pass_states(): slices = lax.all_to_all(local, 'seq', 0, 0, tiled=True)  8.89 us
    all_gather x1, waiting for transfers between devices, per_device(): full_weight = lax.all_gather(out_weight, 'seq', axis=0, tiled=True)  8.44 us
    unnamed x12, other arithmetic  7.76 us
  transfers between devices with their start and end apart: 14, of which 7 were waited for; matrix products, arithmetic and copies ran while one was open for 24% of the time, Pallas kernels for 9%

profile of v2, /device:TPU:11, one launch (start us, length us, event | category | flops | bytes accessed | tf_op | source)
XLA Modules:
  0.0 237.6 jit_solution(965112746188270865)
XLA Ops:
  10.0 4.6 %all-to-all-start = ((f32[8,1,32]{2,1,0:T(1,128)}), f32[8,1,32]{2,1,0:T(1,128)S(1)}, u32[]{:S(2)}, u32[]{:S(2)}) async-start(f32[8,1,32]{2,1,0:T(1,128)} %broadcast_in_dim.49), calls=%async_computation | async-start | bytes 8192 | tf_op jit(solution)/shard_map/all_to_all | solution.py:279
  14.6 3.1 %shard_map.144 = (bf16[128,2048]{1,0:T(8,128)(2,1)}, f32[2,24,256]{2,1,0:T(8,128)S(1)}, f32[2,256,24]{2,1,0:T(8,128)S(1)}) custom-call(f32[2,24,256]{2,1,0:T(8,128)S(1)} %pad_maximum_fusion.decay_ref, bf16[256,2048]{1,0:T(8,128)(2,1)S(1)} %copy-done.4, bf16[256,256]{1,0:T(8,128)(2,1)S(1)} %copy-done.7), custom_call_target="tpu_custom_call" | custom-call | flops 268435456 | bytes 8388608 | tf_op jit(solution)/shard_map/pallas_call | solution.py:207
  17.7 4.8 %all-to-all-start.1 = ((bf16[8,16,2048]{2,1,0:T(8,128)(2,1)}), bf16[8,16,2048]{2,1,0:T(8,128)(2,1)S(1)}, u32[]{:S(2)}, u32[]{:S(2)}) async-start(bf16[8,16,2048]{2,1,0:T(8,128)(2,1)} %bitcast.2), calls=%async_computation.1 | async-start | bytes 1048576 | tf_op jit(solution)/shard_map/all_to_all | solution.py:223
  22.8 1.3 collective-permute-start
  24.1 1.1 collective-permute-start.1
  25.2 1.4 collective-permute-start.2
  28.2 6.2 %all-to-all-done.1 = bf16[8,16,2048]{2,1,0:T(8,128)(2,1)S(1)} async-done(((bf16[8,16,2048]{2,1,0:T(8,128)(2,1)}), bf16[8,16,2048]{2,1,0:T(8,128)(2,1)S(1)}, u32[]{:S(2)}, u32[]{:S(2)}) %all-to-all-start.1) | async-done | bytes 524320 | tf_op jit(solution)/shard_map/all_to_all | solution.py:223
  39.1 7.3 %all-to-all-start.2 = ((bf16[8,16,2048]{2,1,0:T(8,128)(2,1)}), bf16[8,16,2048]{2,1,0:T(8,128)(2,1)S(1)}, u32[]{:S(2)}, u32[]{:S(2)}) async-start(bf16[8,16,2048]{2,1,0:T(8,128)(2,1)} %bitcast.16), calls=%async_computation.2 | async-start | bytes 1048576 | tf_op jit(solution)/shard_map/all_to_all | solution.py:232
  46.4 1.5 broadcast_in_dim.64
  48.6 1.9 constant_dynamic-update-slice_fusion.4
  50.5 18.3 %collective-permute-done.1 = bf16[256,1024]{0,1:T(8,128)(2,1)} collective-permute-done((bf16[256,1024]{0,1:T(8,128)(2,1)S(1)}, bf16[256,1024]{0,1:T(8,128)(2,1)}, u32[]{:S(2)}, u32[]{:S(2)}) %collective-permute-start.1) | collective-permute-done | bytes 524320 | tf_op jit(solution)/shard_map/ppermute | solution.py:237
  68.8 1.9 constant_dynamic-update-slice_fusion.3
  72.2 4.8 %all-to-all-start.3 = ((bf16[256,8,512]{0,2,1:T(8,128)(2,1)}), bf16[256,8,512]{0,2,1:T(8,128)(2,1)}, u32[]{:S(2)}, u32[]{:S(2)}) async-start(bf16[256,8,512]{0,2,1:T(8,128)(2,1)} %bitcast.19), calls=%async_computation.3 | async-start | bytes 4194304 | tf_op jit(solution)/shard_map/all_to_all | solution.py:276
  77.1 4.8 %shard_map.145 = (f32[256,2048]{1,0:T(8,128)}, bf16[256,2048]{1,0:T(8,128)(2,1)}) custom-call(bf16[256,2048]{1,0:T(8,128)(2,1)S(1)} %copy-done.4, bf16[256,256]{1,0:T(8,128)(2,1)S(1)} %copy-done.7, bf16[256,256]{1,0:T(8,128)(2,1)S(1)} %copy-done.2, bf16[256,2048]{1,0:T(8,128)(2,1)S(1)} %copy-done.1, f32[2,24,256]{2,1,0:T(8,128)S(1)} %get-tuple-element.22.cum_ref, ...), custom_call_target="tpu_custom_call" | custom-call | flops 805306368 | bytes 8388608 | tf_op jit(solution)/shard_map/pallas_call | solution.py:207
  81.9 40.7 %all-to-all-done.3 = bf16[256,8,512]{0,2,1:T(8,128)(2,1)} async-done(((bf16[256,8,512]{0,2,1:T(8,128)(2,1)}), bf16[256,8,512]{0,2,1:T(8,128)(2,1)}, u32[]{:S(2)}, u32[]{:S(2)}) %all-to-all-start.3) | async-done | bytes 2097184 | tf_op jit(solution)/shard_map/all_to_all | solution.py:276
  122.6 3.9 %copy.20 = bf16[8,256,512]{2,1,0:T(8,128)(2,1)} copy(bf16[8,256,512]{1,2,0:T(8,128)(2,1)} %bitcast.20) | data formatting | bytes 4194304 | tf_op jit(solution)/shard_map/all_to_all | solution.py:276
  126.6 8.4 %all-gather.3.cloned.1.call-done = bf16[4096,2048]{1,0:T(8,128)(2,1)} async-done(((bf16[512,2048]{1,0:T(8,128)(2,1)}), bf16[4096,2048]{1,0:T(8,128)(2,1)}) %all-gather.3.cloned.1.call-update) | async-done | bytes 16777232 | tf_op jit(solution)/shard_map/all_gather | solution.py:274
  135.2 4.6 %fusion.14 = bf16[256,1024]{1,0:T(8,128)(2,1)} fusion(bf16[256,2048]{1,0:T(8,128)(2,1)} %get-tuple-element.36, bf16[4096,2048]{1,0:T(8,128)(2,1)} %all-gather.3.cloned.1.call-done, s32[]{:T(128)S(6)} %select_n.68), kind=kOutput, calls=%fused_computation.10 | convolution fusion | flops 1074003968 | bytes 5767172 | tf_op jit(solution)/shard_map/dot_general | solution.py:21
  140.1 13.4 %fusion.60.grad_ref = f32[256,2048]{1,0:T(8,128)} fusion(bf16[256,4096]{0,1:T(8,128)(2,1)} %constant_dynamic-update-slice_fusion.2, bf16[4096,2048]{1,0:T(8,128)(2,1)} %all-gather.3.cloned.1.call-done), kind=kOutput, calls=%fused_computation.83 | convolution fusion | flops 4294967296 | bytes 20971520 | tf_op jit(solution)/shard_map/dot_general | solution.py:21
  153.5 4.7 %shard_map.146 = (bf16[256,2048]{1,0:T(8,128)(2,1)S(1)}, f32[256,2048]{1,0:T(8,128)}, bf16[128,2048]{1,0:T(8,128)(2,1)}) custom-call(f32[256,2048]{1,0:T(8,128)S(1)} %copy-done, bf16[256,2048]{1,0:T(8,128)(2,1)S(1)} %copy-done.1, f32[1,2048]{1,0:T(1,128)S(1)} %bitcast.143, f32[256,2048]{1,0:T(8,128)} %fusion.60.grad_ref, bf16[256,256]{1,0:T(8,128)(2,1)S(1)} %copy-done.2, ...), custom_call_target="tpu_custom_call" | custom-call | flops 268435456 | bytes 8388608 | tf_op jit(solution)/shard_map/pallas_call | solution.py:207
  159.2 4.1 %all-to-all-start.4 = ((bf16[8,16,2048]{2,1,0:T(8,128)(2,1)}), bf16[8,16,2048]{2,1,0:T(8,128)(2,1)S(1)}, u32[]{:S(2)}, u32[]{:S(2)}) async-start(bf16[8,16,2048]{2,1,0:T(8,128)(2,1)} %bitcast.23), calls=%async_computation.4 | async-start | bytes 1048576 | tf_op jit(solution)/shard_map/all_to_all | solution.py:223
  163.3 5.2 %fusion.11 = bf16[256,1024]{1,0:T(8,128)(2,1)} fusion(bf16[256,2048]{1,0:T(8,128)(2,1)} %get-tuple-element.36, bf16[4096,2048]{1,0:T(8,128)(2,1)} %all-gather.3.cloned.1.call-done, s32[]{:T(128)S(6)} %select_n.66), kind=kOutput, calls=%fused_computation.9 | convolution fusion | flops 1074003968 | bytes 5767172 | tf_op jit(solution)/shard_map/dot_general | solution.py:21
  168.5 2.1 collective-permute-start.4
  170.6 4.6 %fusion.8 = bf16[256,1024]{1,0:T(8,128)(2,1)} fusion(bf16[256,2048]{1,0:T(8,128)(2,1)} %get-tuple-element.36, bf16[4096,2048]{1,0:T(8,128)(2,1)} %all-gather.3.cloned.1.call-done, s32[]{:T(128)S(6)} %select_n.64), kind=kOutput, calls=%fused_computation.8 | convolution fusion | flops 1074003968 | bytes 5767172 | tf_op jit(solution)/shard_map/dot_general | solution.py:21
  175.2 1.2 collective-permute-start.3
  181.6 5.5 %all-to-all-start.5 = ((bf16[8,16,2048]{2,1,0:T(8,128)(2,1)}), bf16[8,16,2048]{2,1,0:T(8,128)(2,1)S(1)}, u32[]{:S(2)}, u32[]{:S(2)}) async-start(bf16[8,16,2048]{2,1,0:T(8,128)(2,1)} %bitcast.31), calls=%async_computation.5 | async-start | bytes 1048576 | tf_op jit(solution)/shard_map/all_to_all | solution.py:232
  187.1 6.8 %collective-permute-done.4 = bf16[256,1024]{1,0:T(8,128)(2,1)S(1)} collective-permute-done((bf16[256,1024]{1,0:T(8,128)(2,1)}, bf16[256,1024]{1,0:T(8,128)(2,1)S(1)}, u32[]{:S(2)}, u32[]{:S(2)}) %collective-permute-start.4) | collective-permute-done | bytes 524320 | tf_op jit(solution)/shard_map/ppermute | solution.py:237
  193.9 11.2 %collective-permute-done.3 = bf16[256,1024]{1,0:T(8,128)(2,1)} collective-permute-done((bf16[256,1024]{1,0:T(8,128)(2,1)}, bf16[256,1024]{1,0:T(8,128)(2,1)}, u32[]{:S(2)}, u32[]{:S(2)}) %collective-permute-start.3) | collective-permute-done | bytes 524320 | tf_op jit(solution)/shard_map/ppermute | solution.py:237
  205.1 4.9 %add_convert_fusion = bf16[256,1024]{1,0:T(8,128)(2,1)} fusion(bf16[256,1024]{1,0:T(8,128)(2,1)} %collective-permute-done.5, bf16[256,1024]{1,0:T(8,128)(2,1)S(1)} %collective-permute-done.4, bf16[256,1024]{1,0:T(8,128)(2,1)} %collective-permute-done.3, bf16[256,2048]{1,0:T(8,128)(2,1)} %get-tuple-element.36, ...), kind=kOutput, calls=%fused_computation.13 | convolution fusion | flops 1076101120 | bytes 7340036 | tf_op jit(solution)/shard_map/dot_general | solution.py:21
  210.0 1.2 copy-done.6
  211.2 8.9 %shard_map.147 = (f32[256,2048]{1,0:T(8,128)}, f32[256,256]{1,0:T(8,128)}, f32[256,256]{1,0:T(8,128)}, f32[32,256]{1,0:T(8,128)}) custom-call(bf16[256,2048]{1,0:T(8,128)(2,1)S(1)} %copy-done.4, bf16[256,256]{1,0:T(8,128)(2,1)S(1)} %copy-done.7, bf16[256,256]{1,0:T(8,128)(2,1)S(1)} %copy-done.2, bf16[256,2048]{1,0:T(8,128)(2,1)S(1)} %copy-done.6, ...), custom_call_target="tpu_custom_call" | custom-call | flops 2684354560 | bytes 8388608 | tf_op jit(solution)/shard_map/pallas_call | solution.py:207
  220.1 10.6 %fusion.61 = f32[512,2048]{1,0:T(8,128)} fusion(bf16[2048,512]{1,0:T(8,128)(2,1)} %bitcast.144, bf16[2048,2048]{1,0:T(8,128)(2,1)} %all-gather.5.cloned.1.call-done), kind=kOutput, calls=%fused_computation.84 | convolution fusion | flops 4294967296 | bytes 14680064 | tf_op jit(solution)/shard_map/dot_general | solution.py:21
  (78 shorter events, 17.6 us)
Async XLA Ops:
  7.2 0.8 copy-start.10
  7.2 2.1 copy-start.9
  7.2 7.4 %copy-start.4 = (bf16[256,2048]{1,0:T(8,128)(2,1)S(1)}, bf16[256,2048]{1,0:T(8,128)(2,1)}, u32[]{:S(2)}) copy-start(bf16[256,2048]{1,0:T(8,128)(2,1)} %x_ref.5) | copy-start | bytes 3145732
  7.2 7.4 %copy-start.7 = (bf16[256,256]{1,0:T(8,128)(2,1)S(1)}, bf16[256,256]{1,0:T(8,128)(2,1)}, u32[]{:S(2)}) copy-start(bf16[256,256]{1,0:T(8,128)(2,1)} %b_ref.5) | copy-start | bytes 393220
  7.2 127.8 %all-gather.3.cloned.1.call-start = ((), (), s32[]{:S(2)}) async-start(), calls=%async_computation.6 | async-start | bytes 18874368 | tf_op jit(solution)/shard_map/all_gather | solution.py:274
  10.0 7.8 %all-to-all-start = ((f32[8,1,32]{2,1,0:T(1,128)}), f32[8,1,32]{2,1,0:T(1,128)S(1)}, u32[]{:S(2)}, u32[]{:S(2)}) async-start(f32[8,1,32]{2,1,0:T(1,128)} %broadcast_in_dim.49), calls=%async_computation | async-start | bytes 8192 | tf_op jit(solution)/shard_map/all_to_all | solution.py:279
  14.6 8.0 %copy-start.8 = (bf16[256,1024]{1,0:T(8,128)(2,1)S(1)}, bf16[256,1024]{1,0:T(8,128)(2,1)}, u32[]{:S(2)}) copy-start(bf16[256,1024]{1,0:T(8,128)(2,1)} %param.17) | copy-start | bytes 1572868
  17.7 16.7 %all-to-all-start.1 = ((bf16[8,16,2048]{2,1,0:T(8,128)(2,1)}), bf16[8,16,2048]{2,1,0:T(8,128)(2,1)S(1)}, u32[]{:S(2)}, u32[]{:S(2)}) async-start(bf16[8,16,2048]{2,1,0:T(8,128)(2,1)} %bitcast.2), calls=%async_computation.1 | async-start | bytes 1048576 | tf_op jit(solution)/shard_map/all_to_all | solution.py:223
  22.8 25.9 %collective-permute-start = (bf16[256,1024]{0,1:T(8,128)(2,1)S(1)}, bf16[256,1024]{0,1:T(8,128)(2,1)}, u32[]{:S(2)}, u32[]{:S(2)}) collective-permute-start(bf16[256,1024]{0,1:T(8,128)(2,1)S(1)} %copy.16), channel_id=1, source_target_pairs={{0,1},{1,2},{2,3},{3,0},{4,5},{5,6},{6,7},{7,4},{8,9},{9,10},{10,1... | collective-permute-start | bytes 1572872 | tf_op jit(solution)/shard_map/ppermute | solution.py:237
  24.1 44.7 %collective-permute-start.1 = (bf16[256,1024]{0,1:T(8,128)(2,1)S(1)}, bf16[256,1024]{0,1:T(8,128)(2,1)}, u32[]{:S(2)}, u32[]{:S(2)}) collective-permute-start(bf16[256,1024]{0,1:T(8,128)(2,1)S(1)} %copy.16), channel_id=1, source_target_pairs={{0,2},{1,3},{2,0},{3,1},{4,6},{5,7},{6,4},{7,5},{8,10},{9,11},{10,... | collective-permute-start | bytes 1572872 | tf_op jit(solution)/shard_map/ppermute | solution.py:237
  25.2 46.2 %collective-permute-start.2 = (bf16[256,1024]{0,1:T(8,128)(2,1)S(1)}, bf16[256,1024]{0,1:T(8,128)(2,1)S(1)}, u32[]{:S(2)}, u32[]{:S(2)}) collective-permute-start(bf16[256,1024]{0,1:T(8,128)(2,1)S(1)} %copy.16), channel_id=1, source_target_pairs={{0,3},{1,0},{2,1},{3,2},{4,7},{5,4},{6,5},{7,6},{8,11},{9,8},{10,9... | collective-permute-start | bytes 1572872 | tf_op jit(solution)/shard_map/ppermute | solution.py:237
  39.1 33.1 %all-to-all-start.2 = ((bf16[8,16,2048]{2,1,0:T(8,128)(2,1)}), bf16[8,16,2048]{2,1,0:T(8,128)(2,1)S(1)}, u32[]{:S(2)}, u32[]{:S(2)}) async-start(bf16[8,16,2048]{2,1,0:T(8,128)(2,1)} %bitcast.16), calls=%async_computation.2 | async-start | bytes 1048576 | tf_op jit(solution)/shard_map/all_to_all | solution.py:232
  72.2 4.9 %copy-start.1 = (bf16[256,2048]{1,0:T(8,128)(2,1)S(1)}, bf16[256,2048]{1,0:T(8,128)(2,1)}, u32[]{:S(2)}) copy-start(bf16[256,2048]{1,0:T(8,128)(2,1)} %z_ref.3) | copy-start | bytes 3145732
  72.2 4.9 %copy-start.2 = (bf16[256,256]{1,0:T(8,128)(2,1)S(1)}, bf16[256,256]{1,0:T(8,128)(2,1)}, u32[]{:S(2)}) copy-start(bf16[256,256]{1,0:T(8,128)(2,1)} %c_ref.5) | copy-start | bytes 393220
  72.2 4.9 %copy-start.3 = (f32[2048]{0:T(1024)S(1)}, f32[2048]{0:T(1024)}, u32[]{:S(2)}) copy-start(f32[2048]{0:T(1024)} %param.15) | copy-start | bytes 24580
  72.2 50.4 %all-to-all-start.3 = ((bf16[256,8,512]{0,2,1:T(8,128)(2,1)}), bf16[256,8,512]{0,2,1:T(8,128)(2,1)}, u32[]{:S(2)}, u32[]{:S(2)}) async-start(bf16[256,8,512]{0,2,1:T(8,128)(2,1)} %bitcast.19), calls=%async_computation.3 | async-start | bytes 4194304 | tf_op jit(solution)/shard_map/all_to_all | solution.py:276
  77.1 143.1 %all-gather.5.cloned.1.call-start = ((), (), s32[]{:S(2)}) async-start(), calls=%async_computation.7 | async-start | bytes 9437184 | tf_op jit(solution)/shard_map/all_gather | solution.py:305
  139.8 13.7 %copy-start = (f32[256,2048]{1,0:T(8,128)S(1)}, f32[256,2048]{1,0:T(8,128)}, u32[]{:S(2)}) copy-start(f32[256,2048]{1,0:T(8,128)} %get-tuple-element.27.y_ref) | copy-start | bytes 6291460
  139.8 47.3 %collective-permute-start.5 = (bf16[256,1024]{1,0:T(8,128)(2,1)}, bf16[256,1024]{1,0:T(8,128)(2,1)}, u32[]{:S(2)}, u32[]{:S(2)}) collective-permute-start(bf16[256,1024]{1,0:T(8,128)(2,1)} %fusion.14), channel_id=1, source_target_pairs={{0,3},{1,0},{2,1},{3,2},{4,7},{5,4},{6,5},{7,6},{8,11},{9,8},{10,9... | collective-permute-start | bytes 1572872 | tf_op jit(solution)/shard_map/ppermute | solution.py:237
  158.3 1.0 copy-start.5
  159.2 17.2 %all-to-all-start.4 = ((bf16[8,16,2048]{2,1,0:T(8,128)(2,1)}), bf16[8,16,2048]{2,1,0:T(8,128)(2,1)S(1)}, u32[]{:S(2)}, u32[]{:S(2)}) async-start(bf16[8,16,2048]{2,1,0:T(8,128)(2,1)} %bitcast.23), calls=%async_computation.4 | async-start | bytes 1048576 | tf_op jit(solution)/shard_map/all_to_all | solution.py:223
  168.5 25.4 %collective-permute-start.4 = (bf16[256,1024]{1,0:T(8,128)(2,1)}, bf16[256,1024]{1,0:T(8,128)(2,1)S(1)}, u32[]{:S(2)}, u32[]{:S(2)}) collective-permute-start(bf16[256,1024]{1,0:T(8,128)(2,1)} %fusion.11), channel_id=1, source_target_pairs={{0,2},{1,3},{2,0},{3,1},{4,6},{5,7},{6,4},{7,5},{8,10},{9,11},{10,... | collective-permute-start | bytes 1572872 | tf_op jit(solution)/shard_map/ppermute | solution.py:237
  175.2 29.9 %collective-permute-start.3 = (bf16[256,1024]{1,0:T(8,128)(2,1)}, bf16[256,1024]{1,0:T(8,128)(2,1)}, u32[]{:S(2)}, u32[]{:S(2)}) collective-permute-start(bf16[256,1024]{1,0:T(8,128)(2,1)} %fusion.8), channel_id=1, source_target_pairs={{0,1},{1,2},{2,3},{3,0},{4,5},{5,6},{6,7},{7,4},{8,9},{9,10},{10,1... | collective-permute-start | bytes 1572872 | tf_op jit(solution)/shard_map/ppermute | solution.py:237
  181.6 28.3 %all-to-all-start.5 = ((bf16[8,16,2048]{2,1,0:T(8,128)(2,1)}), bf16[8,16,2048]{2,1,0:T(8,128)(2,1)S(1)}, u32[]{:S(2)}, u32[]{:S(2)}) async-start(bf16[8,16,2048]{2,1,0:T(8,128)(2,1)} %bitcast.31), calls=%async_computation.5 | async-start | bytes 1048576 | tf_op jit(solution)/shard_map/all_to_all | solution.py:232
  210.0 1.2 copy-start.6
Sparse Core Ops, SparseCore 0:
  9.9 125.0 all-gather.2
  136.9 64.8 all-gather.4

commit v3 on v2

--- a/solution.py
+++ b/solution.py
@@ -252,15 +252,14 @@
     count = lax.axis_size("head")
     rows = weight.shape[0] // count
     me = lax.axis_index("head")
-    total = None
-    for steps in list(range(1, count)) + [0]:
+    terms = []
+    for steps in range(count):
         block = lax.dynamic_slice(
             weight, ((me + steps) % count * rows, 0), (rows, weight.shape[1])
         )
         term = mm(normed, block, NT).astype(BF16)
-        term = (shift(term, steps) if steps else term).astype(F32)
-        total = term if total is None else total + term
-    return total.astype(BF16)
+        terms.append(shift(term, steps) if steps else term)
+    return terms
 
 
 def per_device(
@@ -310,7 +309,7 @@
         ("wide", "wide", "state"), (BF16, F32, BF16), square,
         y, gate_z, gain, grad_y, inputs_c, cum_t,
     )
-    layer_out = project(normed_bf, full_weight)
+    terms = project(normed_bf, full_weight)
     adjoint_out = pass_states(adjoint, decays, True)
     grad_x, grad_b, grad_c, grad_decay = run(
         scan_grad_kernel, groups, tokens,
@@ -318,6 +317,8 @@
         ("wide", "narrow", "narrow", "heads"), (F32, F32, F32, F32), 10 * square,
         inputs_x, inputs_b, inputs_c, dy, cum, cum_t, state_in, adjoint_out,
     )
+    terms, grad_decay = lax.optimization_barrier((terms, grad_decay))
+    layer_out = sum(term.astype(F32) for term in terms).astype(BF16)
     grad_weight = mm(grad_columns, normed_all, TN)
     return (layer_out, grad_x, grad_b, grad_c, grad_z, grad_decay, grad_weight)
 

time: 241 us -> 232 us (0.963)
  waiting for transfers between devices: 93 us -> 85.5 us
  other arithmetic: 9.36 us -> 11.8 us
    ppermute x6, waiting for transfers between devices: 37 us -> 28.7 us  [shift(): lax.ppermute(value, 'head', [(i, (i + steps) % count) for i in range(coun...]
  transfers between devices with their start and end apart: 14 -> 14, of which waited for: 7 -> 8; matrix products, arithmetic and copies ran while one was open for 24% -> 25% of each run, Pallas kernels for 9% -> 9%
where the time goes in v3:
time: 232 us; the launch traced here: 230 us
  waiting for transfers between devices  85.5 us (37%)
  matrix products  41.6 us (18%)
  starting transfers between devices  38 us (16%)
  Pallas kernels  21.6 us (9%)
  local copies, waits for them, and re-layouts  16.9 us (7%)
  between operations  14.9 us (6%)
  other arithmetic  11.8 us (5%)
    dot_general x6, matrix products, mm(): return lax.dot_general(a, b, dims, preferred_element_type=F32)  41.6 us
    all_to_all x1, waiting for transfers between devices, per_device(): grad_columns = lax.all_to_all(grad_full, 'seq', 1, 0, tiled=True)  40.7 us
    ppermute x6, waiting for transfers between devices, shift(): lax.ppermute(value, 'head', [(i, (i + steps) % count) for i in range(coun...  28.7 us
    pallas_call x4, Pallas kernels, run(): pl.pallas_call(kernel, grid=(groups,), in_specs=group_specs([(k, tokens)...  21.6 us
    all_to_all x2, starting transfers between devices, pass_states(): lax.all_to_all(jnp.concatenate(incoming, axis=0), 'seq', 0, 0, tiled=True)  12.1 us
    all_to_all x2, starting transfers between devices, pass_states(): slices = lax.all_to_all(local, 'seq', 0, 0, tiled=True)  8.66 us
    all_gather x1, waiting for transfers between devices, per_device(): full_weight = lax.all_gather(out_weight, 'seq', axis=0, tiled=True)  8.43 us
    unnamed x12, other arithmetic  7.85 us
  transfers between devices with their start and end apart: 14, of which 8 were waited for; matrix products, arithmetic and copies ran while one was open for 25% of the time, Pallas kernels for 9%

profile of v3, /device:TPU:11, one launch (start us, length us, event | category | flops | bytes accessed | tf_op | source)
XLA Modules:
  0.0 230.3 jit_solution(8790431992578441654)
XLA Ops:
  10.0 4.6 %all-to-all-start = ((f32[8,1,32]{2,1,0:T(1,128)}), f32[8,1,32]{2,1,0:T(1,128)S(1)}, u32[]{:S(2)}, u32[]{:S(2)}) async-start(f32[8,1,32]{2,1,0:T(1,128)} %broadcast_in_dim.49), calls=%async_computation | async-start | bytes 8192 | tf_op jit(solution)/shard_map/all_to_all | solution.py:278
  14.6 3.1 %shard_map.144 = (bf16[128,2048]{1,0:T(8,128)(2,1)}, f32[2,24,256]{2,1,0:T(8,128)S(1)}, f32[2,256,24]{2,1,0:T(8,128)S(1)}) custom-call(f32[2,24,256]{2,1,0:T(8,128)S(1)} %pad_maximum_fusion.decay_ref, bf16[256,2048]{1,0:T(8,128)(2,1)S(1)} %copy-done.4, bf16[256,256]{1,0:T(8,128)(2,1)S(1)} %copy-done.7), custom_call_target="tpu_custom_call" | custom-call | flops 268435456 | bytes 8388608 | tf_op jit(solution)/shard_map/pallas_call | solution.py:207
  17.7 4.8 %all-to-all-start.1 = ((bf16[8,16,2048]{2,1,0:T(8,128)(2,1)}), bf16[8,16,2048]{2,1,0:T(8,128)(2,1)S(1)}, u32[]{:S(2)}, u32[]{:S(2)}) async-start(bf16[8,16,2048]{2,1,0:T(8,128)(2,1)} %bitcast.2), calls=%async_computation.1 | async-start | bytes 1048576 | tf_op jit(solution)/shard_map/all_to_all | solution.py:223
  22.8 1.3 collective-permute-start
  25.2 1.4 collective-permute-start.2
  28.2 6.2 %all-to-all-done.1 = bf16[8,16,2048]{2,1,0:T(8,128)(2,1)S(1)} async-done(((bf16[8,16,2048]{2,1,0:T(8,128)(2,1)}), bf16[8,16,2048]{2,1,0:T(8,128)(2,1)S(1)}, u32[]{:S(2)}, u32[]{:S(2)}) %all-to-all-start.1) | async-done | bytes 524320 | tf_op jit(solution)/shard_map/all_to_all | solution.py:223
  39.1 7.3 %all-to-all-start.2 = ((bf16[8,16,2048]{2,1,0:T(8,128)(2,1)}), bf16[8,16,2048]{2,1,0:T(8,128)(2,1)S(1)}, u32[]{:S(2)}, u32[]{:S(2)}) async-start(bf16[8,16,2048]{2,1,0:T(8,128)(2,1)} %bitcast.16), calls=%async_computation.2 | async-start | bytes 1048576 | tf_op jit(solution)/shard_map/all_to_all | solution.py:232
  46.4 1.5 broadcast_in_dim.64
  48.7 1.9 constant_dynamic-update-slice_fusion.4
  50.5 18.2 %collective-permute-done.1 = bf16[256,1024]{0,1:T(8,128)(2,1)} collective-permute-done((bf16[256,1024]{0,1:T(8,128)(2,1)S(1)}, bf16[256,1024]{0,1:T(8,128)(2,1)}, u32[]{:S(2)}, u32[]{:S(2)}) %collective-permute-start.1) | collective-permute-done | bytes 524320 | tf_op jit(solution)/shard_map/ppermute | solution.py:237
  68.8 1.9 constant_dynamic-update-slice_fusion.3
  72.2 4.9 %all-to-all-start.3 = ((bf16[256,8,512]{0,2,1:T(8,128)(2,1)}), bf16[256,8,512]{0,2,1:T(8,128)(2,1)}, u32[]{:S(2)}, u32[]{:S(2)}) async-start(bf16[256,8,512]{0,2,1:T(8,128)(2,1)} %bitcast.19), calls=%async_computation.3 | async-start | bytes 4194304 | tf_op jit(solution)/shard_map/all_to_all | solution.py:275
  77.1 4.8 %shard_map.145 = (f32[256,2048]{1,0:T(8,128)}, bf16[256,2048]{1,0:T(8,128)(2,1)}) custom-call(bf16[256,2048]{1,0:T(8,128)(2,1)S(1)} %copy-done.4, bf16[256,256]{1,0:T(8,128)(2,1)S(1)} %copy-done.7, bf16[256,256]{1,0:T(8,128)(2,1)S(1)} %copy-done.2, bf16[256,2048]{1,0:T(8,128)(2,1)S(1)} %copy-done.1, f32[2,24,256]{2,1,0:T(8,128)S(1)} %get-tuple-element.27.cum_ref, ...), custom_call_target="tpu_custom_call" | custom-call | flops 805306368 | bytes 8388608 | tf_op jit(solution)/shard_map/pallas_call | solution.py:207
  81.9 40.7 %all-to-all-done.3 = bf16[256,8,512]{0,2,1:T(8,128)(2,1)} async-done(((bf16[256,8,512]{0,2,1:T(8,128)(2,1)}), bf16[256,8,512]{0,2,1:T(8,128)(2,1)}, u32[]{:S(2)}, u32[]{:S(2)}) %all-to-all-start.3) | async-done | bytes 2097184 | tf_op jit(solution)/shard_map/all_to_all | solution.py:275
  122.6 3.9 %copy.20 = bf16[8,256,512]{2,1,0:T(8,128)(2,1)} copy(bf16[8,256,512]{1,2,0:T(8,128)(2,1)} %bitcast.20) | data formatting | bytes 4194304 | tf_op jit(solution)/shard_map/all_to_all | solution.py:275
  126.6 8.4 %all-gather.3.cloned.1.call-done = bf16[4096,2048]{1,0:T(8,128)(2,1)} async-done(((bf16[512,2048]{1,0:T(8,128)(2,1)}), bf16[4096,2048]{1,0:T(8,128)(2,1)}) %all-gather.3.cloned.1.call-update) | async-done | bytes 16777232 | tf_op jit(solution)/shard_map/all_gather | solution.py:273
  135.2 12.4 %fusion.55.grad_ref = f32[256,2048]{1,0:T(8,128)} fusion(bf16[256,4096]{0,1:T(8,128)(2,1)} %constant_dynamic-update-slice_fusion.2, bf16[4096,2048]{1,0:T(8,128)(2,1)} %all-gather.3.cloned.1.call-done), kind=kOutput, calls=%fused_computation.82 | convolution fusion | flops 4294967296 | bytes 20971520 | tf_op jit(solution)/shard_map/dot_general | solution.py:21
  147.6 4.7 %shard_map.146 = (bf16[256,2048]{1,0:T(8,128)(2,1)S(1)}, f32[256,2048]{1,0:T(8,128)}, bf16[128,2048]{1,0:T(8,128)(2,1)}) custom-call(f32[256,2048]{1,0:T(8,128)S(1)} %copy-done, bf16[256,2048]{1,0:T(8,128)(2,1)S(1)} %copy-done.1, f32[1,2048]{1,0:T(1,128)S(1)} %bitcast.143, f32[256,2048]{1,0:T(8,128)} %fusion.55.grad_ref, bf16[256,256]{1,0:T(8,128)(2,1)S(1)} %copy-done.2, ...), custom_call_target="tpu_custom_call" | custom-call | flops 268435456 | bytes 8388608 | tf_op jit(solution)/shard_map/pallas_call | solution.py:207
  153.3 3.8 %all-to-all-start.4 = ((bf16[8,16,2048]{2,1,0:T(8,128)(2,1)}), bf16[8,16,2048]{2,1,0:T(8,128)(2,1)S(1)}, u32[]{:S(2)}, u32[]{:S(2)}) async-start(bf16[8,16,2048]{2,1,0:T(8,128)(2,1)} %bitcast.23), calls=%async_computation.4 | async-start | bytes 1048576 | tf_op jit(solution)/shard_map/all_to_all | solution.py:223
  157.1 4.6 %fusion.11 = bf16[256,1024]{1,0:T(8,128)(2,1)} fusion(bf16[256,2048]{1,0:T(8,128)(2,1)} %get-tuple-element.46, bf16[4096,2048]{1,0:T(8,128)(2,1)} %all-gather.3.cloned.1.call-done, s32[]{:T(128)S(6)} %select_n.64), kind=kOutput, calls=%fused_computation.9 | convolution fusion | flops 1074003968 | bytes 5767172 | tf_op jit(solution)/shard_map/dot_general | solution.py:21
  161.7 1.2 collective-permute-start.3
  162.9 4.8 %fusion.14 = bf16[256,1024]{1,0:T(8,128)(2,1)} fusion(bf16[256,2048]{1,0:T(8,128)(2,1)} %get-tuple-element.46, bf16[4096,2048]{1,0:T(8,128)(2,1)} %all-gather.3.cloned.1.call-done, s32[]{:T(128)S(6)} %select_n.66), kind=kOutput, calls=%fused_computation.10 | convolution fusion | flops 1074003968 | bytes 5767172 | tf_op jit(solution)/shard_map/dot_general | solution.py:21
  174.0 4.8 %all-to-all-start.5 = ((bf16[8,16,2048]{2,1,0:T(8,128)(2,1)}), bf16[8,16,2048]{2,1,0:T(8,128)(2,1)S(1)}, u32[]{:S(2)}, u32[]{:S(2)}) async-start(bf16[8,16,2048]{2,1,0:T(8,128)(2,1)} %bitcast.31), calls=%async_computation.5 | async-start | bytes 1048576 | tf_op jit(solution)/shard_map/all_to_all | solution.py:232
  178.8 4.6 %fusion.17 = bf16[256,1024]{1,0:T(8,128)(2,1)} fusion(bf16[256,2048]{1,0:T(8,128)(2,1)} %get-tuple-element.46, bf16[4096,2048]{1,0:T(8,128)(2,1)} %all-gather.3.cloned.1.call-done, s32[]{:T(128)S(6)} %select_n.68), kind=kOutput, calls=%fused_computation.11 | convolution fusion | flops 1074003968 | bytes 5767172 | tf_op jit(solution)/shard_map/dot_general | solution.py:21
  183.3 1.9 collective-permute-start.5
  185.2 4.6 %fusion.8 = bf16[256,1024]{1,0:T(8,128)(2,1)} fusion(bf16[256,2048]{1,0:T(8,128)(2,1)} %get-tuple-element.46, bf16[4096,2048]{1,0:T(8,128)(2,1)} %all-gather.3.cloned.1.call-done, s32[]{:T(128)S(6)} %select_n.56), kind=kOutput, calls=%fused_computation.8 | convolution fusion | flops 1074003968 | bytes 5767172 | tf_op jit(solution)/shard_map/dot_general | solution.py:21
  190.6 1.2 copy-done.6
  191.8 8.9 %shard_map.147 = (f32[256,2048]{1,0:T(8,128)}, f32[256,256]{1,0:T(8,128)}, f32[256,256]{1,0:T(8,128)}, f32[32,256]{1,0:T(8,128)}) custom-call(bf16[256,2048]{1,0:T(8,128)(2,1)S(1)} %copy-done.4, bf16[256,256]{1,0:T(8,128)(2,1)S(1)} %copy-done.7, bf16[256,256]{1,0:T(8,128)(2,1)S(1)} %copy-done.2, bf16[256,2048]{1,0:T(8,128)(2,1)S(1)} %copy-done.6, ...), custom_call_target="tpu_custom_call" | custom-call | flops 2684354560 | bytes 8388608 | tf_op jit(solution)/shard_map/pallas_call | solution.py:207
  200.8 7.1 %collective-permute-done.4 = bf16[256,1024]{1,0:T(8,128)(2,1)} collective-permute-done((bf16[256,1024]{1,0:T(8,128)(2,1)}, bf16[256,1024]{1,0:T(8,128)(2,1)}, u32[]{:S(2)}, u32[]{:S(2)}) %collective-permute-start.4) | collective-permute-done | bytes 524320 | tf_op jit(solution)/shard_map/ppermute | solution.py:237
  207.9 2.6 %collective-permute-done.5 = bf16[256,1024]{1,0:T(8,128)(2,1)} collective-permute-done((bf16[256,1024]{1,0:T(8,128)(2,1)}, bf16[256,1024]{1,0:T(8,128)(2,1)}, u32[]{:S(2)}, u32[]{:S(2)}) %collective-permute-start.5) | collective-permute-done | bytes 524320 | tf_op jit(solution)/shard_map/ppermute | solution.py:237
  210.5 2.4 %add_convert_fusion = bf16[256,1024]{1,0:T(8,128)(2,1)} fusion(bf16[256,1024]{1,0:T(8,128)(2,1)} %collective-permute-done.5, bf16[256,1024]{1,0:T(8,128)(2,1)} %collective-permute-done.4, bf16[256,1024]{1,0:T(8,128)(2,1)S(1)} %collective-permute-done.3, bf16[256,1024]{1,0:T(8,128)(2,1)S(1)} %copy-done.8), kind=kLoop, calls=%fused_computation.12 | loop fusion | flops 2097152 | bytes 2621440 | tf_op jit(solution)/shard_map/convert_element_type | solution.py:321
  212.9 10.6 %fusion.56 = f32[512,2048]{1,0:T(8,128)} fusion(bf16[2048,512]{1,0:T(8,128)(2,1)} %bitcast.144, bf16[2048,2048]{1,0:T(8,128)(2,1)} %all-gather.5.cloned.1.call-done), kind=kOutput, calls=%fused_computation.83 | convolution fusion | flops 4294967296 | bytes 14680064 | tf_op jit(solution)/shard_map/dot_general | solution.py:21
  (81 shorter events, 20.2 us)
Async XLA Ops:
  7.2 0.8 copy-start.11
  7.2 2.1 copy-start.10
  7.2 7.4 %copy-start.4 = (bf16[256,2048]{1,0:T(8,128)(2,1)S(1)}, bf16[256,2048]{1,0:T(8,128)(2,1)}, u32[]{:S(2)}) copy-start(bf16[256,2048]{1,0:T(8,128)(2,1)} %x_ref.5) | copy-start | bytes 3145732
  7.2 7.4 %copy-start.7 = (bf16[256,256]{1,0:T(8,128)(2,1)S(1)}, bf16[256,256]{1,0:T(8,128)(2,1)}, u32[]{:S(2)}) copy-start(bf16[256,256]{1,0:T(8,128)(2,1)} %b_ref.5) | copy-start | bytes 393220
  7.2 127.8 %all-gather.3.cloned.1.call-start = ((), (), s32[]{:S(2)}) async-start(), calls=%async_computation.6 | async-start | bytes 18874368 | tf_op jit(solution)/shard_map/all_gather | solution.py:273
  10.0 7.8 %all-to-all-start = ((f32[8,1,32]{2,1,0:T(1,128)}), f32[8,1,32]{2,1,0:T(1,128)S(1)}, u32[]{:S(2)}, u32[]{:S(2)}) async-start(f32[8,1,32]{2,1,0:T(1,128)} %broadcast_in_dim.49), calls=%async_computation | async-start | bytes 8192 | tf_op jit(solution)/shard_map/all_to_all | solution.py:278
  14.6 8.0 %copy-start.9 = (bf16[256,1024]{1,0:T(8,128)(2,1)S(1)}, bf16[256,1024]{1,0:T(8,128)(2,1)}, u32[]{:S(2)}) copy-start(bf16[256,1024]{1,0:T(8,128)(2,1)} %param.17) | copy-start | bytes 1572868
  17.7 16.7 %all-to-all-start.1 = ((bf16[8,16,2048]{2,1,0:T(8,128)(2,1)}), bf16[8,16,2048]{2,1,0:T(8,128)(2,1)S(1)}, u32[]{:S(2)}, u32[]{:S(2)}) async-start(bf16[8,16,2048]{2,1,0:T(8,128)(2,1)} %bitcast.2), calls=%async_computation.1 | async-start | bytes 1048576 | tf_op jit(solution)/shard_map/all_to_all | solution.py:223
  22.8 25.9 %collective-permute-start = (bf16[256,1024]{0,1:T(8,128)(2,1)S(1)}, bf16[256,1024]{0,1:T(8,128)(2,1)}, u32[]{:S(2)}, u32[]{:S(2)}) collective-permute-start(bf16[256,1024]{0,1:T(8,128)(2,1)S(1)} %copy.16), channel_id=1, source_target_pairs={{0,1},{1,2},{2,3},{3,0},{4,5},{5,6},{6,7},{7,4},{8,9},{9,10},{10,1... | collective-permute-start | bytes 1572872 | tf_op jit(solution)/shard_map/ppermute | solution.py:237
  24.1 44.7 %collective-permute-start.1 = (bf16[256,1024]{0,1:T(8,128)(2,1)S(1)}, bf16[256,1024]{0,1:T(8,128)(2,1)}, u32[]{:S(2)}, u32[]{:S(2)}) collective-permute-start(bf16[256,1024]{0,1:T(8,128)(2,1)S(1)} %copy.16), channel_id=1, source_target_pairs={{0,2},{1,3},{2,0},{3,1},{4,6},{5,7},{6,4},{7,5},{8,10},{9,11},{10,... | collective-permute-start | bytes 1572872 | tf_op jit(solution)/shard_map/ppermute | solution.py:237
  25.2 46.2 %collective-permute-start.2 = (bf16[256,1024]{0,1:T(8,128)(2,1)S(1)}, bf16[256,1024]{0,1:T(8,128)(2,1)S(1)}, u32[]{:S(2)}, u32[]{:S(2)}) collective-permute-start(bf16[256,1024]{0,1:T(8,128)(2,1)S(1)} %copy.16), channel_id=1, source_target_pairs={{0,3},{1,0},{2,1},{3,2},{4,7},{5,4},{6,5},{7,6},{8,11},{9,8},{10,9... | collective-permute-start | bytes 1572872 | tf_op jit(solution)/shard_map/ppermute | solution.py:237
  39.1 33.1 %all-to-all-start.2 = ((bf16[8,16,2048]{2,1,0:T(8,128)(2,1)}), bf16[8,16,2048]{2,1,0:T(8,128)(2,1)S(1)}, u32[]{:S(2)}, u32[]{:S(2)}) async-start(bf16[8,16,2048]{2,1,0:T(8,128)(2,1)} %bitcast.16), calls=%async_computation.2 | async-start | bytes 1048576 | tf_op jit(solution)/shard_map/all_to_all | solution.py:232
  72.2 4.9 %copy-start.1 = (bf16[256,2048]{1,0:T(8,128)(2,1)S(1)}, bf16[256,2048]{1,0:T(8,128)(2,1)}, u32[]{:S(2)}) copy-start(bf16[256,2048]{1,0:T(8,128)(2,1)} %z_ref.3) | copy-start | bytes 3145732
  72.2 4.9 %copy-start.2 = (bf16[256,256]{1,0:T(8,128)(2,1)S(1)}, bf16[256,256]{1,0:T(8,128)(2,1)}, u32[]{:S(2)}) copy-start(bf16[256,256]{1,0:T(8,128)(2,1)} %c_ref.5) | copy-start | bytes 393220
  72.2 4.9 %copy-start.3 = (f32[2048]{0:T(1024)S(1)}, f32[2048]{0:T(1024)}, u32[]{:S(2)}) copy-start(f32[2048]{0:T(1024)} %param.15) | copy-start | bytes 24580
  72.2 50.4 %all-to-all-start.3 = ((bf16[256,8,512]{0,2,1:T(8,128)(2,1)}), bf16[256,8,512]{0,2,1:T(8,128)(2,1)}, u32[]{:S(2)}, u32[]{:S(2)}) async-start(bf16[256,8,512]{0,2,1:T(8,128)(2,1)} %bitcast.19), calls=%async_computation.3 | async-start | bytes 4194304 | tf_op jit(solution)/shard_map/all_to_all | solution.py:275
  77.1 135.8 %all-gather.5.cloned.1.call-start = ((), (), s32[]{:S(2)}) async-start(), calls=%async_computation.7 | async-start | bytes 9437184 | tf_op jit(solution)/shard_map/all_gather | solution.py:304
  135.2 12.4 %copy-start = (f32[256,2048]{1,0:T(8,128)S(1)}, f32[256,2048]{1,0:T(8,128)}, u32[]{:S(2)}) copy-start(f32[256,2048]{1,0:T(8,128)} %get-tuple-element.32.y_ref) | copy-start | bytes 6291460
  152.3 1.0 copy-start.5
  153.3 15.4 %all-to-all-start.4 = ((bf16[8,16,2048]{2,1,0:T(8,128)(2,1)}), bf16[8,16,2048]{2,1,0:T(8,128)(2,1)S(1)}, u32[]{:S(2)}, u32[]{:S(2)}) async-start(bf16[8,16,2048]{2,1,0:T(8,128)(2,1)} %bitcast.23), calls=%async_computation.4 | async-start | bytes 1048576 | tf_op jit(solution)/shard_map/all_to_all | solution.py:223
  161.7 39.0 %collective-permute-start.3 = (bf16[256,1024]{1,0:T(8,128)(2,1)}, bf16[256,1024]{1,0:T(8,128)(2,1)S(1)}, u32[]{:S(2)}, u32[]{:S(2)}) collective-permute-start(bf16[256,1024]{1,0:T(8,128)(2,1)} %fusion.11), channel_id=1, source_target_pairs={{0,1},{1,2},{2,3},{3,0},{4,5},{5,6},{6,7},{7,4},{8,9},{9,10},{10,1... | collective-permute-start | bytes 1572872 | tf_op jit(solution)/shard_map/ppermute | solution.py:237
  167.8 40.1 %collective-permute-start.4 = (bf16[256,1024]{1,0:T(8,128)(2,1)}, bf16[256,1024]{1,0:T(8,128)(2,1)}, u32[]{:S(2)}, u32[]{:S(2)}) collective-permute-start(bf16[256,1024]{1,0:T(8,128)(2,1)} %fusion.14), channel_id=1, source_target_pairs={{0,2},{1,3},{2,0},{3,1},{4,6},{5,7},{6,4},{7,5},{8,10},{9,11},{10,... | collective-permute-start | bytes 1572872 | tf_op jit(solution)/shard_map/ppermute | solution.py:237
  174.0 16.6 %all-to-all-start.5 = ((bf16[8,16,2048]{2,1,0:T(8,128)(2,1)}), bf16[8,16,2048]{2,1,0:T(8,128)(2,1)S(1)}, u32[]{:S(2)}, u32[]{:S(2)}) async-start(bf16[8,16,2048]{2,1,0:T(8,128)(2,1)} %bitcast.31), calls=%async_computation.5 | async-start | bytes 1048576 | tf_op jit(solution)/shard_map/all_to_all | solution.py:232
  183.3 27.2 %collective-permute-start.5 = (bf16[256,1024]{1,0:T(8,128)(2,1)}, bf16[256,1024]{1,0:T(8,128)(2,1)}, u32[]{:S(2)}, u32[]{:S(2)}) collective-permute-start(bf16[256,1024]{1,0:T(8,128)(2,1)} %fusion.17), channel_id=1, source_target_pairs={{0,3},{1,0},{2,1},{3,2},{4,7},{5,4},{6,5},{7,6},{8,11},{9,8},{10,9... | collective-permute-start | bytes 1572872 | tf_op jit(solution)/shard_map/ppermute | solution.py:237
  190.6 1.2 copy-start.6
  191.8 18.7 %copy-start.8 = (bf16[256,1024]{1,0:T(8,128)(2,1)S(1)}, bf16[256,1024]{1,0:T(8,128)(2,1)}, u32[]{:S(2)}) copy-start(bf16[256,1024]{1,0:T(8,128)(2,1)} %fusion.8) | copy-start | bytes 1572868
Sparse Core Ops, SparseCore 0:
  9.9 125.0 all-gather.2
  136.9 59.9 all-gather.4
